TPU v7x, 256 devices: a whole 4x4x8 slice. The times are simulated.
256 devices in a mesh: fsdp: 64 (over z, x_hi, y), tensor: 4 (over x_lo, core).
Axes of the slice: x: 4 (x_hi: 2, x_lo: 2; x = x_hi * 2 + x_lo), y: 4, z: 8, core: 2. Of those that a mesh axis runs over, the one named last changes fastest.
Arguments:
- head_out: bfloat16 [32768, 3072], P('fsdp', 'tensor'), may hold values from -6 to 6
- stream: bfloat16 [32768, 4608], P('fsdp', 'tensor'), may hold values from -100 to 100
- tangent: bfloat16 [4608, 3072], P('fsdp', 'tensor'), may hold values from -2 to 2
- norm_gain: bfloat16 [4608], P('tensor'), may hold values from 0.099609375 to 1.8984375
- curvature: float32 [32768], P('fsdp'), may hold values from 0.001171875 to 0.01171875
- kept_counts: int32 [128], P('fsdp'), may hold values from 64 to 192, as said below
Outputs:
- curvature_product: float32 [4608, 3072], P('fsdp', 'tensor')
- normed_tangent: bfloat16 [32768, 4608], P('fsdp', 'tensor')
Inputs may be any that keep to these rules, and one draw needn't show every extreme that they name: `kept_counts`: in every draw the 2 images of some index of fsdp each keep 192 patches.
All inputs are finite; a program needn't handle non-finite values.
Results may differ from a plain program's by a relative error of at most 0.015.
Values may be sent and summed in bfloat16 or wider, within the bound.
No kernel may reach another device: no remote copies, remote signals or barrier semaphores. Data moves between devices by JAX's collectives and lax.ppermute only.
A program may use at most 128 MiB of HBM per device.

v0:
```python
import functools

import jax
import jax.numpy as jnp
from jax import lax
from jax.experimental import pallas as pl
from jax.experimental.pallas import tpu as pltpu
from jax.sharding import Mesh
from jax.sharding import PartitionSpec as P

SLOTS = 256
KEEP_MOST = 192
EPS = 1e-06

SIZES = {"z": 8, "h": 2, "y": 4, "l": 2, "c": 2}
ALL = tuple(SIZES)
FSDP = ("z", "h", "y")
TENSOR = ("l", "c")
XRING = ("h", "l")
LIMIT = 24 * 1024 * 1024


def flat(z, h, y, t):
    return ((z * 2 + h) * 4 + y) * 4 + t


THERE = [
    (flat(z, h, y, t), flat(2 * ((t + z // 2) % 4) + z % 2, h, y, z // 2))
    for z in range(8)
    for h in range(2)
    for y in range(4)
    for t in range(4)
]
BACK = [(b, a) for a, b in THERE]


def shift(x, axis, by):
    n = 4 if axis == XRING else SIZES[axis]
    return lax.ppermute(x, axis, [(i, (i + by) % n) for i in range(n)])


def after(first, *rest):
    return lax.optimization_barrier((first,) + rest)[1:]


def call(kernel, outs, flops, place, heads, *args):
    moved = sum(a.size * a.dtype.itemsize for a in (heads,) + args)
    moved += sum(o.size * o.dtype.itemsize for o in outs)
    _, rows, features = heads.shape

    def body(place_ref, *refs):
        pieces, rest = refs[0], refs[1:-2]
        whole, sems = refs[-2:]
        copies = [
            pltpu.make_async_copy(
                pieces.at[(i % 2 ^ place_ref[2]) * 4 + i // 2],
                whole.at[i // 2, pl.ds((i % 2) * rows, rows)],
                sems.at[i],
            )
            for i in range(8)
        ]
        for copy in copies:
            copy.start()
        kernel(place_ref, (whole, copies), *rest)

    return pl.pallas_call(
        body,
        out_shape=outs,
        in_specs=[pl.BlockSpec(memory_space=pltpu.SMEM)]
        + [pl.BlockSpec(memory_space=pl.ANY)]
        + [pl.BlockSpec(memory_space=pltpu.VMEM)] * len(args),
        out_specs=[pl.BlockSpec(memory_space=pltpu.VMEM)] * len(outs),
        scratch_shapes=[
            pltpu.VMEM((4, 2 * rows, features), jnp.bfloat16),
            pltpu.SemaphoreType.DMA((8,)),
        ],
        compiler_params=pltpu.CompilerParams(vmem_limit_bytes=LIMIT),
        cost_estimate=pl.CostEstimate(flops=flops, bytes_accessed=moved, transcendentals=0),
    )(place, heads, *args)


def arrive(heads):
    whole, copies = heads
    for copy in copies:
        copy.wait()
    return whole


def group(place, offset):
    return lax.rem(lax.rem(place[0] + offset + 8, 8) // 2 - place[1] + 4, 4)


def add_pieces(offsets, place, heads, pieces, halves):
    for i, offset in enumerate(offsets):
        piece = pieces[i][...]
        if offset == 4:
            piece = jnp.concatenate([piece, pieces[i + 1][...]], axis=0)
        term = lax.dot_general(
            piece,
            heads[group(place, offset)],
            (((1,), (1,)), ((), ())),
            preferred_element_type=jnp.float32,
        )
        k = offset % 2
        halves[k] = term if halves[k] is None else halves[k] + term
    return halves


def early_kernel(offsets, z_ref, heads, values_ref, own, far, near, beyond, *refs):
    pieces, (change_ref, xhat_ref, row_ref) = refs[:-3], refs[-3:]
    rows = own.shape[2] // 2

    def swapped(x):
        return jnp.concatenate([x[:, rows:], x[:, :rows]], axis=1)

    parts = [own[0], own[1], near[0], near[1]]
    parts += [swapped(x[i]) for x in (far, beyond) for i in range(2)]
    mean = sum(p[0:1] for p in parts) * 0.125
    square = sum(p[1:2] + jnp.square(p[0:1] - mean) for p in parts) * 0.125
    scale = lax.rsqrt(square + EPS)
    weights = jnp.concatenate([own[0][2:3, :rows], far[0][2:3, rows:]], axis=1)
    row_ref[...] = jnp.concatenate([weights, scale], axis=0)
    for k in range(2):
        xhat_ref[k] = (values_ref[k] - mean) * scale
    halves = add_pieces(offsets, z_ref, arrive(heads), pieces, [None, None])
    change_ref[0] = halves[0]
    change_ref[1] = halves[1]


def late_kernel(offsets, z_ref, heads, early, xhat_ref, gain_ref, *refs):
    pieces, (change_ref, sums_ref) = refs[:-2], refs[-2:]
    halves = add_pieces(offsets, z_ref, arrive(heads), pieces, [early[0], early[1]])
    total = jnp.zeros((8, change_ref.shape[2]), jnp.float32)
    rows = []
    for k in range(2):
        change_ref[k] = halves[k]
        xhat = xhat_ref[k]
        gain = gain_ref[k]
        gain2 = gain * gain
        raised = gain2 * halves[k]
        lifted = gain2 * xhat
        parts = [
            halves[k],
            halves[k] * xhat,
            raised,
            raised * xhat,
            lifted,
            lifted * xhat,
            jnp.broadcast_to(gain2, xhat.shape),
        ]
        rows.append([jnp.sum(p, axis=0, keepdims=True) for p in parts])
    for i, (a, b) in enumerate(zip(*rows)):
        sums_ref[pl.ds(i, 1), :] = a + b
    sums_ref[pl.ds(7, 1), :] = total[:1]


def back_kernel(width, z_ref, heads, change_ref, xhat_ref, gain_ref, row_ref, *refs):
    sums, (back_ref, normed_ref), terms = refs[:4], refs[4:6], refs[6:]
    total = sum(s[...] for s in sums) * (1.0 / width)
    mean_change, mean_hat, mean_up, mean_up_hat, gain_hat, gain_hat2, gain_mean = (
        total[i : i + 1] for i in range(7)
    )
    weights, scale = row_ref[0:1, :], row_ref[1:2, :]
    factor = weights * scale
    first = factor * (mean_up - mean_change * gain_mean - mean_hat * gain_hat)
    second = factor * (mean_up_hat - mean_change * gain_hat - mean_hat * gain_hat2)
    for k in range(2):
        gain, xhat = gain_ref[k], xhat_ref[k]
        normed = gain * (change_ref[k] - mean_change - xhat * mean_hat) * scale
        normed_ref[k] = normed.astype(normed_ref.dtype)
        lifted = gain * weights * normed
        back_ref[k] = ((lifted - first - xhat * second) * scale).astype(back_ref.dtype)
    multiply((4, 3, -3), z_ref, arrive(heads), back_ref, terms)


def multiply(offsets, place, heads, back_ref, outs):
    for i, offset in enumerate(offsets):
        term = jnp.dot(
            back_ref[offset % 2], heads[group(place, offset)], preferred_element_type=jnp.float32
        )
        if len(outs) == len(offsets):
            outs[i][...] = term
            continue
        middle = term.shape[0] // 2
        outs[2 * i][...] = term[:middle].astype(outs[2 * i].dtype)
        outs[2 * i + 1][...] = term[middle:].astype(outs[2 * i + 1].dtype)


def terms_kernel(offsets, z_ref, heads, back_ref, *outs):
    multiply(offsets, z_ref, arrive(heads), back_ref, outs)


def on_device(head_out, stream, tangent, norm_gain, curvature, kept_counts):
    images = kept_counts.shape[0]
    rows = images * KEEP_MOST
    features = head_out.shape[1]
    columns = stream.shape[1]
    half = columns // 2
    quarter = half // 2
    height = tangent.shape[0]
    middle = 2 * height
    width = columns * 4
    z, h, y, l, c = (lax.axis_index(name) for name in ALL)
    odd = z % 2
    f32, bf16 = jnp.float32, jnp.bfloat16

    live = lax.broadcasted_iota(jnp.int32, (images, SLOTS), 1) < kept_counts[:, None]
    weight = jnp.where(live, curvature.reshape(images, SLOTS), 0.0)[:, :KEEP_MOST].reshape(rows)
    head = head_out.reshape(images, SLOTS, features)[:, :KEEP_MOST].reshape(rows, features)
    hidden = stream.reshape(images, SLOTS, columns)[:, :KEEP_MOST].reshape(rows, columns)

    chunks = hidden.T.reshape(2, 2, 4, height, rows)
    own_half = lax.dynamic_index_in_dim(chunks, h, 1, keepdims=False)
    other_half = lax.dynamic_index_in_dim(chunks, 1 - h, 1, keepdims=False)

    block = lax.ppermute(tangent, ALL, THERE)
    block, own_half, other_half = lax.optimization_barrier((block, own_half, other_half))
    blocks = [block] + [shift(block, "y", by) for by in range(1, 4)]
    got_half = shift(other_half, "h", 1)
    *blocks, got_half = lax.optimization_barrier((*blocks, got_half))
    piece = jnp.concatenate(blocks, axis=0)
    (head,) = after(got_half, head)
    gathered = lax.all_gather(head, XRING + ("c",), axis=0)

    def flip(x, axes, by):
        n = 4 if axes == XRING else 2
        return lax.ppermute(x, axes, [(i, i ^ by) for i in range(n)])

    up, down = [piece], [piece]

    def step(*carried):
        ring = [shift(up[-1], "z", 1), shift(down[-1], "z", -1)]
        got = lax.optimization_barrier((*ring, *carried))
        up.append(got[0])
        down.append(got[1])
        return got[2:]

    step()

    def turned(x):
        x = jnp.where(odd == 0, x, x[::-1])
        x = [lax.dynamic_index_in_dim(x, (y - d) % 4, 1, keepdims=False) for d in range(4)]
        return jnp.concatenate(x, axis=1)

    values = turned(jnp.concatenate([own_half, got_half], axis=-1)).astype(f32)
    gain = norm_gain.reshape(2, 2, 4, height).astype(f32)
    gain = turned(lax.dynamic_index_in_dim(gain, h, 1, keepdims=False)[..., None])

    part_mean = jnp.mean(values, axis=(0, 1))
    part_square = jnp.mean(jnp.square(values - part_mean), axis=(0, 1))

    def swapped(x):
        return jnp.concatenate([x[..., rows:], x[..., :rows]], axis=-1)

    def around(x):
        got = [flip(x, XRING, by) for by in (2, 1, 3)]
        return [x, swapped(got[0]), got[1], swapped(got[2])]

    stats = jnp.stack([part_mean, part_square, jnp.concatenate([weight, weight])])
    (beside,) = step(flip(stats, "c", 1))
    stats = jnp.stack([stats, beside])
    x2, x1, x3 = step(*(flip(stats, XRING, by) for by in (2, 1, 3)))
    across = [shift(up[3][:middle], "z", 1), shift(down[3][middle:], "z", -1)]
    (gathered,) = after(up[2], gathered)
    place = jnp.stack([z, 2 * l + c, h]).astype(jnp.int32)
    shape = (2, quarter, 2 * rows)
    one = 2 * quarter * features * 2 * rows
    early, xhat, scalars = call(
        functools.partial(early_kernel, (0, -1, 1, -2, 2)),
        [
            jax.ShapeDtypeStruct(shape, f32),
            jax.ShapeDtypeStruct(shape, f32),
            jax.ShapeDtypeStruct((2, 2 * rows), f32),
        ],
        5 * one,
        place,
        gathered,
        values,
        stats,
        x2,
        x1,
        x3,
        piece,
        up[1],
        down[1],
        up[2],
        down[2],
    )
    change, sums = call(
        functools.partial(late_kernel, (-3, 3, 4)),
        [jax.ShapeDtypeStruct(shape, f32), jax.ShapeDtypeStruct((8, 2 * rows), f32)],
        3 * one,
        place,
        gathered,
        early,
        xhat,
        gain,
        up[3],
        down[3],
        *across,
    )
    sums = sums + flip(sums, "c", 1)
    half_shape = (middle, features)
    back, normed, *ready = call(
        functools.partial(back_kernel, width),
        [
            jax.ShapeDtypeStruct(shape, bf16),
            jax.ShapeDtypeStruct(shape, bf16),
            *[jax.ShapeDtypeStruct(half_shape, bf16)] * 2,
            *[jax.ShapeDtypeStruct(half_shape, f32)] * 4,
        ],
        3 * one,
        place,
        gathered,
        change,
        xhat,
        gain,
        scalars,
        *around(sums),
    )

    first = {(1, 0): shift(ready[0], "z", 1), (-1, 1): shift(ready[1], "z", -1)}
    (held,) = after(first[1, 0], back)
    offsets = (2, -2, 1, -1, 0)
    terms = call(
        functools.partial(terms_kernel, offsets),
        [jax.ShapeDtypeStruct((quarter, features), f32)] * 5,
        5 * one,
        place,
        gathered,
        held,
    )

    def term(offset, k=None):
        if k is None:
            return terms[offsets.index(offset)]
        return ready[2 * (3, -3).index(offset) + k + 2]

    up = jnp.concatenate([first[1, 0].astype(f32) + term(3, 0), term(3, 1)], axis=0)
    down = jnp.concatenate([term(-3, 0), first[-1, 1].astype(f32) + term(-3, 1)], axis=0)
    for step in (2, 1, 0):
        up = shift(up.astype(bf16), "z", 1).astype(f32)
        down = shift(down.astype(bf16), "z", -1).astype(f32)
        if step:
            up, down = up + term(step), down + term(-step)
    total = up + down + term(0)
    total = [total[i * height : (i + 1) * height] for i in range(4)]
    product = total[0] + sum(shift(total[d].astype(bf16), "y", -d).astype(f32) for d in range(1, 4))
    product = lax.ppermute(product.astype(bf16), ALL, BACK).astype(f32)

    normed = normed.reshape(2, 4, height, 2 * rows)
    normed = [lax.dynamic_index_in_dim(normed, (y - d) % 4, 1, keepdims=False) for d in range(4)]
    normed = jnp.stack(normed, axis=1)
    normed = jnp.where(odd == 0, normed, normed[::-1])
    kept, sent = normed[..., :rows], normed[..., rows:]
    got = shift(sent, "h", 1)
    both = jnp.stack([jnp.where(h == 0, kept, got), jnp.where(h == 0, got, kept)], axis=1)
    both = both.reshape(columns, rows).T
    both = both.reshape(images, KEEP_MOST, columns)
    both = jnp.where(live[:, :KEEP_MOST, None], both, 0).astype(bf16)
    both = jnp.pad(both, ((0, 0), (0, SLOTS - KEEP_MOST), (0, 0)))
    return product, both.reshape(images * SLOTS, columns)


def solution(mesh):
    fine = Mesh(mesh.devices.reshape(tuple(SIZES.values())), ALL)
    placed = (
        P(FSDP, TENSOR),
        P(FSDP, TENSOR),
        P(FSDP, TENSOR),
        P(TENSOR),
        P(FSDP),
        P(FSDP),
    )
    return jax.shard_map(
        on_device,
        mesh=fine,
        in_specs=placed,
        out_specs=(P(FSDP, TENSOR), P(FSDP, TENSOR)),
        check_vma=False,
    )
```

profile of v0, /device:TPU:6, one launch (start us, length us, event | category | flops | bytes accessed | tf_op | source)
XLA Modules:
  0.0 175.1 jit_solution(5541806485855220190)
XLA Ops:
  7.2 9.4 %collective-permute-start = (bf16[72,768]{1,0:T(8,128)(2,1)}, bf16[72,768]{1,0:T(8,128)(2,1)S(1)}, u32[]{:S(2)}, u32[]{:S(2)}) collective-permute-start(bf16[72,768]{1,0:T(8,128)(2,1)} %param.8), channel_id=1, source_target_pairs={{0,0},{1,64},{2,128},{3,192},{4,4},{5,68},{6,132},{7,196},{8,8},{9... | collective-permute-start | bytes 331784 | tf_op jit(solution)/shard_map/ppermute | solution.py:216
  16.6 1.2 slice.67
  17.8 0.9 copy.22
  18.9 0.5 collective-permute-done
  19.4 1.4 collective-permute-start.4
  20.7 1.6 collective-permute-start.1
  22.3 2.9 %collective-permute-start.2 = (bf16[72,768]{1,0:T(8,128)(2,1)S(1)}, bf16[72,768]{1,0:T(8,128)(2,1)S(1)}, u32[]{:S(2)}, u32[]{:S(2)}) collective-permute-start(bf16[72,768]{1,0:T(8,128)(2,1)S(1)} %collective-permute-done), channel_id=1, source_target_pairs={{0,8},{4,12},{8,0},{12,4},{1,9},{5,13},{9,1},{13,5},{2,10},{6,14},... | collective-permute-start | bytes 331784 | tf_op jit(solution)/shard_map/ppermute | solution.py:39
  25.2 1.3 collective-permute-start.3
  26.6 0.9 slice.70
  27.4 3.6 %collective-permute-done.2 = bf16[72,768]{1,0:T(8,128)(2,1)S(1)} collective-permute-done((bf16[72,768]{1,0:T(8,128)(2,1)S(1)}, bf16[72,768]{1,0:T(8,128)(2,1)S(1)}, u32[]{:S(2)}, u32[]{:S(2)}) %collective-permute-start.2) | collective-permute-done | bytes 110624 | tf_op jit(solution)/shard_map/ppermute | solution.py:39
  31.1 1.8 %collective-permute-done.4 = bf16[2,4,72,384]{3,2,1,0:T(8,128)(2,1)S(1)} collective-permute-done((bf16[2,4,72,384]{3,2,1,0:T(8,128)(2,1)S(1)}, bf16[2,4,72,384]{3,2,1,0:T(8,128)(2,1)S(1)}, u32[]{:S(2)}, u32[]{:S(2)}) %collective-permute-start.4) | collective-permute-done | bytes 442400 | tf_op jit(solution)/shard_map/ppermute | solution.py:39
  33.5 1.6 collective-permute-start.5
  35.1 1.7 collective-permute-start.6
  37.6 10.1 %collective-permute-done.5.refs_7_ = bf16[288,768]{1,0:T(8,128)(2,1)S(1)} collective-permute-done((bf16[288,768]{1,0:T(8,128)(2,1)S(1)}, bf16[288,768]{1,0:T(8,128)(2,1)S(1)}, u32[]{:S(2)}, u32[]{:S(2)}) %collective-permute-start.5) | collective-permute-done | bytes 442400 | tf_op jit(solution)/shard_map/ppermute | solution.py:39
  47.8 3.2 %collective-permute-start.8 = (bf16[288,768]{1,0:T(8,128)(2,1)S(1)}, bf16[288,768]{1,0:T(8,128)(2,1)S(1)}, u32[]{:S(2)}, u32[]{:S(2)}) collective-permute-start(bf16[288,768]{1,0:T(8,128)(2,1)S(1)} %collective-permute-done.6.refs_8_), channel_id=1, source_target_pairs={{0,224},{32,0},{64,32},{96,64},{128,96},{160,128},{192,160},{224,1... | collective-permute-start | bytes 1327112 | tf_op jit(solution)/shard_map/ppermute | solution.py:39
  51.2 1.1 collective-permute-done.9
  52.3 8.8 %collective-permute-done.7.refs_9_ = bf16[288,768]{1,0:T(8,128)(2,1)S(1)} collective-permute-done((bf16[288,768]{1,0:T(8,128)(2,1)S(1)}, bf16[288,768]{1,0:T(8,128)(2,1)S(1)}, u32[]{:S(2)}, u32[]{:S(2)}) %collective-permute-start.7) | collective-permute-done | bytes 442400 | tf_op jit(solution)/shard_map/ppermute | solution.py:39
  61.2 3.2 %collective-permute-start.11 = (bf16[288,768]{1,0:T(8,128)(2,1)S(1)}, bf16[288,768]{1,0:T(8,128)(2,1)S(1)}, u32[]{:S(2)}, u32[]{:S(2)}) collective-permute-start(bf16[288,768]{1,0:T(8,128)(2,1)S(1)} %collective-permute-done.8.refs_10_), channel_id=1, source_target_pairs={{0,224},{32,0},{64,32},{96,64},{128,96},{160,128},{192,160},{224,1... | collective-permute-start | bytes 1327112 | tf_op jit(solution)/shard_map/ppermute | solution.py:39
  64.4 0.8 copy-done.7
  65.3 1.2 collective-permute-start.12
  66.9 2.6 %collective-permute-start.14 = (f32[2,3,768]{2,1,0:T(4,128)S(1)}, f32[2,3,768]{2,1,0:T(4,128)S(1)}, u32[]{:S(2)}, u32[]{:S(2)}) collective-permute-start(f32[2,3,768]{2,1,0:T(4,128)S(1)} %pad_maximum_fusion.4.refs_2_), channel_id=1, source_target_pairs={{0,18},{2,16},{16,2},{18,0},{1,19},{3,17},{17,3},{19,1},{4,22},{6,... | collective-permute-start | bytes 55304 | tf_op jit(solution)/shard_map/ppermute | solution.py:227
  69.7 1.0 collective-permute-done.12.refs_3_
  70.7 1.2 collective-permute-done.14.refs_5_
  71.9 1.8 %collective-permute-done.10.refs_4_ = bf16[288,768]{1,0:T(8,128)(2,1)S(1)} collective-permute-done((bf16[288,768]{1,0:T(8,128)(2,1)S(1)}, bf16[288,768]{1,0:T(8,128)(2,1)S(1)}, u32[]{:S(2)}, u32[]{:S(2)}) %collective-permute-start.10) | collective-permute-done | bytes 442400 | tf_op jit(solution)/shard_map/ppermute | solution.py:39
  73.7 0.7 slice.54
  74.5 0.7 slice.55
  75.2 3.3 %collective-permute-start.16 = (bf16[144,768]{1,0:T(8,128)(2,1)}, bf16[144,768]{1,0:T(8,128)(2,1)}, u32[]{:S(2)}, u32[]{:S(2)}) collective-permute-start(bf16[144,768]{1,0:T(8,128)(2,1)} %slice.55), channel_id=1, source_target_pairs={{0,224},{32,0},{64,32},{96,64},{128,96},{160,128},{192,160},{224,1... | collective-permute-start | bytes 663560 | tf_op jit(solution)/shard_map/ppermute | solution.py:39
  78.5 1.4 maximum_convert_fusion.refs_1_
  79.9 2.3 %copy-done = bf16[3072,768]{1,0:T(8,128)(2,1)S(1)} copy-done((bf16[3072,768]{1,0:T(8,128)(2,1)S(1)}, bf16[3072,768]{1,0:T(8,128)(2,1)}, u32[]{:S(2)}) %copy-start) | copy-done | bytes 4718616
  82.3 1.0 copy-done.2
  83.3 1.0 copy-done.4
  84.3 1.0 copy-done.6
  85.3 1.0 copy-done.8
  86.3 3.7 %shard_map.77 = (f32[2,288,768]{2,1,0:T(8,128)S(1)}, f32[2,288,768]{2,1,0:T(8,128)S(1)}, f32[2,768]{1,0:T(2,128)S(1)}) custom-call(s32[3]{0:T(128)S(1)} %pad_add_fusion.place_ref, bf16[8,384,768]{2,1,0:T(8,128)(2,1)S(1)} %bitcast.45, f32[2,288,768]{2,1,0:T(8,128)S(1)} %maximum_convert_fusion.refs_1_, f32[2,3,768]{2,1,0:T(4,128)S(1)} %pad_maximum_fusion.4.refs_2_, ...), custom_call_target="tpu_custom_call" | custom-call | flops 1698693120 | bytes 12318720 | tf_op jit(solution)/shard_map/pallas_call | solution.py:66
  90.1 3.7 %shard_map.78 = (f32[2,288,768]{2,1,0:T(8,128)S(1)}, f32[8,768]{1,0:T(8,128)S(1)}) custom-call(s32[3]{0:T(128)S(1)} %pad_add_fusion.place_ref, bf16[8,384,768]{2,1,0:T(8,128)(2,1)S(1)} %bitcast.46, f32[2,288,768]{2,1,0:T(8,128)S(1)} %get-tuple-element.59.refs_1_, f32[2,288,768]{2,1,0:T(8,128)S(1)} %get-tuple-element.60.refs_2_, ...), custom_call_target="tpu_custom_call" | custom-call | flops 1019215872 | bytes 11380992 | tf_op jit(solution)/shard_map/pallas_call | solution.py:66
  93.9 1.2 collective-permute-done.17
  95.1 0.8 collective-permute-start.18
  95.9 3.0 %collective-permute-start.20 = (f32[8,768]{1,0:T(8,128)S(1)}, f32[8,768]{1,0:T(8,128)S(1)}, u32[]{:S(2)}, u32[]{:S(2)}) collective-permute-start(f32[8,768]{1,0:T(8,128)S(1)} %add.112.refs_5_), channel_id=1, source_target_pairs={{0,18},{2,16},{16,2},{18,0},{1,19},{3,17},{17,3},{19,1},{4,22},{6,... | collective-permute-start | bytes 73736 | tf_op jit(solution)/shard_map/ppermute | solution.py:227
  98.9 1.5 collective-permute-done.18
  100.4 0.5 collective-permute-done.20
  101.0 1.7 collective-permute-done.19.refs_7_
  102.7 3.6 %shard_map.79 = (bf16[2,288,768]{2,1,0:T(8,128)(2,1)S(1)}, bf16[2,288,768]{2,1,0:T(8,128)(2,1)S(1)}, bf16[144,768]{1,0:T(8,128)(2,1)S(1)}, bf16[144,768]{1,0:T(8...) custom-call(s32[3]{0:T(128)S(1)} %pad_add_fusion.place_ref, ...), custom_call_target="tpu_custom_call" | custom-call | flops 1019215872 | bytes 12345600 | tf_op jit(solution)/shard_map/pallas_call | solution.py:66
  106.4 3.3 %collective-permute-start.25 = (bf16[144,768]{1,0:T(8,128)(2,1)S(1)}, bf16[144,768]{1,0:T(8,128)(2,1)S(1)}, u32[]{:S(2)}, u32[]{:S(2)}) collective-permute-start(bf16[144,768]{1,0:T(8,128)(2,1)S(1)} %get-tuple-element.74), channel_id=1, source_target_pairs={{0,224},{32,0},{64,32},{96,64},{128,96},{160,128},{192,160},{224,1... | collective-permute-start | bytes 663560 | tf_op jit(solution)/shard_map/ppermute | solution.py:39
  109.8 3.7 %collective-permute-done.21 = bf16[144,768]{1,0:T(8,128)(2,1)S(1)} collective-permute-done((bf16[144,768]{1,0:T(8,128)(2,1)S(1)}, bf16[144,768]{1,0:T(8,128)(2,1)S(1)}, u32[]{:S(2)}, u32[]{:S(2)}) %collective-permute-start.21) | collective-permute-done | bytes 221216 | tf_op jit(solution)/shard_map/ppermute | solution.py:39
  113.8 3.5 %collective-permute-start.26 = (bf16[288,768]{1,0:T(8,128)(2,1)S(1)}, bf16[288,768]{1,0:T(8,128)(2,1)S(1)}, u32[]{:S(2)}, u32[]{:S(2)}) collective-permute-start(bf16[288,768]{1,0:T(8,128)(2,1)S(1)} %pad_maximum_fusion.3), channel_id=1, source_target_pairs={{0,224},{32,0},{64,32},{96,64},{128,96},{160,128},{192,160},{224,1... | collective-permute-start | bytes 1327112 | tf_op jit(solution)/shard_map/ppermute | solution.py:39
  117.4 3.5 %shard_map.80 = (f32[288,768]{1,0:T(8,128)S(1)}, f32[288,768]{1,0:T(8,128)S(1)}, f32[288,768]{1,0:T(8,128)S(1)}, f32[288,768]{1,0:T(8,128)S(1)}, f32[288,768]{1,0:T(8,128)S(1)}) custom-call(s32[3]{0:T(128)S(1)} %pad_add_fusion.place_ref, bf16[8,384,768]{2,1,0:T(8,128)(2,1)S(1)} %bitcast.48, bf16[2,288,768]{2,1,0:T(8,128)(2,1)S(1)} %get-tuple-element.70.refs_1_), custom_call_target="tpu_custom_call" | custom-call | flops 1698693120 | bytes 10027008 | tf_op jit(solution)/shard_map/pallas_call | solution.py:66
  120.9 3.3 %collective-permute-done.22 = bf16[288,768]{1,0:T(8,128)(2,1)S(1)} collective-permute-done((bf16[288,768]{1,0:T(8,128)(2,1)S(1)}, bf16[288,768]{1,0:T(8,128)(2,1)S(1)}, u32[]{:S(2)}, u32[]{:S(2)}) %collective-permute-start.22) | collective-permute-done | bytes 442400 | tf_op jit(solution)/shard_map/ppermute | solution.py:39
  124.6 3.3 %collective-permute-start.27 = (bf16[288,768]{1,0:T(8,128)(2,1)S(1)}, bf16[288,768]{1,0:T(8,128)(2,1)S(1)}, u32[]{:S(2)}, u32[]{:S(2)}) collective-permute-start(bf16[288,768]{1,0:T(8,128)(2,1)S(1)} %add_convert_fusion.1), channel_id=1, source_target_pairs={{0,224},{32,0},{64,32},{96,64},{128,96},{160,128},{192,160},{224,1... | collective-permute-start | bytes 1327112 | tf_op jit(solution)/shard_map/ppermute | solution.py:39
  128.1 0.8 collective-permute-start.33
  128.8 5.8 %collective-permute-done.23 = bf16[288,768]{1,0:T(8,128)(2,1)S(1)} collective-permute-done((bf16[288,768]{1,0:T(8,128)(2,1)S(1)}, bf16[288,768]{1,0:T(8,128)(2,1)S(1)}, u32[]{:S(2)}, u32[]{:S(2)}) %collective-permute-start.23) | collective-permute-done | bytes 442400 | tf_op jit(solution)/shard_map/ppermute | solution.py:39
  134.9 3.3 %collective-permute-start.28 = (bf16[288,768]{1,0:T(8,128)(2,1)S(1)}, bf16[288,768]{1,0:T(8,128)(2,1)}, u32[]{:S(2)}, u32[]{:S(2)}) collective-permute-start(bf16[288,768]{1,0:T(8,128)(2,1)S(1)} %add_convert_fusion), channel_id=1, source_target_pairs={{0,224},{32,0},{64,32},{96,64},{128,96},{160,128},{192,160},{224,1... | collective-permute-start | bytes 1327112 | tf_op jit(solution)/shard_map/ppermute | solution.py:39
  138.2 1.1 select_bitcast_fusion.1
  139.3 5.0 %collective-permute-done.24 = bf16[288,768]{1,0:T(8,128)(2,1)S(1)} collective-permute-done((bf16[288,768]{1,0:T(8,128)(2,1)S(1)}, bf16[288,768]{1,0:T(8,128)(2,1)S(1)}, u32[]{:S(2)}, u32[]{:S(2)}) %collective-permute-start.24) | collective-permute-done | bytes 442400 | tf_op jit(solution)/shard_map/ppermute | solution.py:39
  144.3 1.1 fusion.3
  145.5 3.1 %collective-permute-start.29 = (bf16[72,768]{1,0:T(8,128)(2,1)S(1)}, bf16[72,768]{1,0:T(8,128)(2,1)S(1)}, u32[]{:S(2)}, u32[]{:S(2)}) collective-permute-start(bf16[72,768]{1,0:T(8,128)(2,1)S(1)} %get-tuple-element.94), channel_id=1, source_target_pairs={{0,12},{4,0},{8,4},{12,8},{1,13},{5,1},{9,5},{13,9},{2,14},{6,2},{... | collective-permute-start | bytes 331784 | tf_op jit(solution)/shard_map/ppermute | solution.py:39
  148.6 0.6 collective-permute-start.30
  149.2 1.0 collective-permute-start.31
  150.3 0.9 copy.26
  151.2 3.7 %collective-permute-done.30 = bf16[72,768]{1,0:T(8,128)(2,1)S(1)} collective-permute-done((bf16[72,768]{1,0:T(8,128)(2,1)S(1)}, bf16[72,768]{1,0:T(8,128)(2,1)S(1)}, u32[]{:S(2)}, u32[]{:S(2)}) %collective-permute-start.30) | collective-permute-done | bytes 110624 | tf_op jit(solution)/shard_map/ppermute | solution.py:39
  154.9 1.1 collective-permute-done.31
  156.1 3.9 %collective-permute-start.32 = (bf16[72,768]{1,0:T(8,128)(2,1)S(1)}, bf16[72,768]{1,0:T(8,128)(2,1)S(1)}, u32[]{:S(2)}, u32[]{:S(2)}) collective-permute-start(bf16[72,768]{1,0:T(8,128)(2,1)S(1)} %fusion), channel_id=1, source_target_pairs={{0,0},{64,1},{128,2},{192,3},{4,4},{68,5},{132,6},{196,7},{8,8},{7... | collective-permute-start | bytes 331784 | tf_op jit(solution)/shard_map/ppermute | solution.py:349
  160.1 1.1 pad.4
  161.2 6.3 %collective-permute-done.32 = bf16[72,768]{1,0:T(8,128)(2,1)S(1)} collective-permute-done((bf16[72,768]{1,0:T(8,128)(2,1)S(1)}, bf16[72,768]{1,0:T(8,128)(2,1)S(1)}, u32[]{:S(2)}, u32[]{:S(2)}) %collective-permute-start.32) | collective-permute-done | bytes 110624 | tf_op jit(solution)/shard_map/ppermute | solution.py:349
  167.5 0.7 convert_element_type.88
  (108 shorter events, 4.3 us)
Async XLA Ops:
  7.2 72.7 %all-gather.3.cloned.1.call-start = ((), (), s32[]{:S(2)}) async-start(), calls=%async_computation | async-start | bytes 5308416 | tf_op jit(solution)/shard_map/all_gather | solution.py:223
  7.2 12.2 %collective-permute-start = (bf16[72,768]{1,0:T(8,128)(2,1)}, bf16[72,768]{1,0:T(8,128)(2,1)S(1)}, u32[]{:S(2)}, u32[]{:S(2)}) collective-permute-start(bf16[72,768]{1,0:T(8,128)(2,1)} %param.8), channel_id=1, source_target_pairs={{0,0},{1,64},{2,128},{3,192},{4,4},{5,68},{6,132},{7,196},{8,8},{9... | collective-permute-start | bytes 331784 | tf_op jit(solution)/shard_map/ppermute | solution.py:216
  17.8 8.7 %copy-start.13 = (bf16[512,768]{1,0:T(8,128)(2,1)S(1)}, bf16[512,768]{1,0:T(8,128)(2,1)}, u32[]{:S(2)}) copy-start(bf16[512,768]{1,0:T(8,128)(2,1)} %param.6) | copy-start | bytes 2359300
  18.7 14.3 %copy-start.15 = (f32[512]{0:T(512)S(1)}, f32[512]{0:T(512)}, u32[]{:S(2)}) copy-start(f32[512]{0:T(512)} %param.10) | copy-start | bytes 6148
  18.7 14.3 %copy-start.16 = (s32[2]{0:T(128)S(1)}, s32[2]{0:T(128)}, u32[]{:S(2)}) copy-start(s32[2]{0:T(128)} %param.11) | copy-start | bytes 28
  18.7 14.5 %copy-start.14 = (bf16[1152]{0:T(1024)(128)(2,1)S(1)}, bf16[1152]{0:T(1024)(128)(2,1)}, u32[]{:S(2)}) copy-start(bf16[1152]{0:T(1024)(128)(2,1)} %param.9) | copy-start | bytes 6916
  19.4 13.5 %collective-permute-start.4 = (bf16[2,4,72,384]{3,2,1,0:T(8,128)(2,1)S(1)}, bf16[2,4,72,384]{3,2,1,0:T(8,128)(2,1)S(1)}, u32[]{:S(2)}, u32[]{:S(2)}) collective-permute-start(bf16[2,4,72,384]{3,2,1,0:T(8,128)(2,1)S(1)} %get-tuple-element.42), channel_id=1, source_target_pairs={{0,16},{16,0},{1,17},{17,1},{2,18},{18,2},{3,19},{19,3},{4,20},{20... | collective-permute-start | bytes 1327112 | tf_op jit(solution)/shard_map/ppermute | solution.py:39
  20.7 6.7 %collective-permute-start.1 = (bf16[72,768]{1,0:T(8,128)(2,1)S(1)}, bf16[72,768]{1,0:T(8,128)(2,1)S(1)}, u32[]{:S(2)}, u32[]{:S(2)}) collective-permute-start(bf16[72,768]{1,0:T(8,128)(2,1)S(1)} %collective-permute-done), channel_id=1, source_target_pairs={{0,4},{4,8},{8,12},{12,0},{1,5},{5,9},{9,13},{13,1},{2,6},{6,10},{... | collective-permute-start | bytes 331784 | tf_op jit(solution)/shard_map/ppermute | solution.py:39
  22.3 8.7 %collective-permute-start.2 = (bf16[72,768]{1,0:T(8,128)(2,1)S(1)}, bf16[72,768]{1,0:T(8,128)(2,1)S(1)}, u32[]{:S(2)}, u32[]{:S(2)}) collective-permute-start(bf16[72,768]{1,0:T(8,128)(2,1)S(1)} %collective-permute-done), channel_id=1, source_target_pairs={{0,8},{4,12},{8,0},{12,4},{1,9},{5,13},{9,1},{13,5},{2,10},{6,14},... | collective-permute-start | bytes 331784 | tf_op jit(solution)/shard_map/ppermute | solution.py:39
  25.2 5.9 %collective-permute-start.3 = (bf16[72,768]{1,0:T(8,128)(2,1)S(1)}, bf16[72,768]{1,0:T(8,128)(2,1)S(1)}, u32[]{:S(2)}, u32[]{:S(2)}) collective-permute-start(bf16[72,768]{1,0:T(8,128)(2,1)S(1)} %collective-permute-done), channel_id=1, source_target_pairs={{0,12},{4,0},{8,4},{12,8},{1,13},{5,1},{9,5},{13,9},{2,14},{6,2},{... | collective-permute-start | bytes 331784 | tf_op jit(solution)/shard_map/ppermute | solution.py:39
  33.5 14.2 %collective-permute-start.5 = (bf16[288,768]{1,0:T(8,128)(2,1)S(1)}, bf16[288,768]{1,0:T(8,128)(2,1)S(1)}, u32[]{:S(2)}, u32[]{:S(2)}) collective-permute-start(bf16[288,768]{1,0:T(8,128)(2,1)S(1)} %constant_dynamic-update-slice_fusion.refs_6_), channel_id=1, source_target_pairs={{0,32},{32,64},{64,96},{96,128},{128,160},{160,192},{192,224},{224... | collective-permute-start | bytes 1327112 | tf_op jit(solution)/shard_map/ppermute | solution.py:39
  35.1 12.6 %collective-permute-start.6 = (bf16[288,768]{1,0:T(8,128)(2,1)S(1)}, bf16[288,768]{1,0:T(8,128)(2,1)S(1)}, u32[]{:S(2)}, u32[]{:S(2)}) collective-permute-start(bf16[288,768]{1,0:T(8,128)(2,1)S(1)} %constant_dynamic-update-slice_fusion.refs_6_), channel_id=1, source_target_pairs={{0,224},{32,0},{64,32},{96,64},{128,96},{160,128},{192,160},{224,1... | collective-permute-start | bytes 1327112 | tf_op jit(solution)/shard_map/ppermute | solution.py:39
  37.1 24.0 %copy-start.10 = (bf16[2,72,768]{2,1,0:T(8,128)(2,1)}, bf16[2,72,768]{2,1,0:T(8,128)(2,1)S(1)}, u32[]{:S(2)}) copy-start(bf16[2,72,768]{2,1,0:T(8,128)(2,1)S(1)} %get-tuple-element.89) | copy-start | bytes 663556
  37.1 23.9 %copy-start.11 = (bf16[2,72,768]{2,1,0:T(8,128)(2,1)}, bf16[2,72,768]{2,1,0:T(8,128)(2,1)S(1)}, u32[]{:S(2)}) copy-start(bf16[2,72,768]{2,1,0:T(8,128)(2,1)S(1)} %get-tuple-element.90) | copy-start | bytes 663556
  37.1 23.9 %copy-start.12 = (bf16[2,72,768]{2,1,0:T(8,128)(2,1)}, bf16[2,72,768]{2,1,0:T(8,128)(2,1)S(1)}, u32[]{:S(2)}) copy-start(bf16[2,72,768]{2,1,0:T(8,128)(2,1)S(1)} %get-tuple-element.91) | copy-start | bytes 663556
  37.2 32.3 %copy-start.9 = (bf16[2,72,768]{2,1,0:T(8,128)(2,1)}, bf16[2,72,768]{2,1,0:T(8,128)(2,1)S(1)}, u32[]{:S(2)}) copy-start(bf16[2,72,768]{2,1,0:T(8,128)(2,1)S(1)} %get-tuple-element.88) | copy-start | bytes 663556
  47.7 27.5 %copy-start.1 = (bf16[288,768]{1,0:T(8,128)(2,1)}, bf16[288,768]{1,0:T(8,128)(2,1)S(1)}, u32[]{:S(2)}) copy-start(bf16[288,768]{1,0:T(8,128)(2,1)S(1)} %collective-permute-done.5.refs_7_) | copy-start | bytes 1327108
  47.7 27.5 %copy-start.3 = (bf16[288,768]{1,0:T(8,128)(2,1)}, bf16[288,768]{1,0:T(8,128)(2,1)S(1)}, u32[]{:S(2)}) copy-start(bf16[288,768]{1,0:T(8,128)(2,1)S(1)} %collective-permute-done.6.refs_8_) | copy-start | bytes 1327108
  47.7 13.4 %collective-permute-start.7 = (bf16[288,768]{1,0:T(8,128)(2,1)S(1)}, bf16[288,768]{1,0:T(8,128)(2,1)S(1)}, u32[]{:S(2)}, u32[]{:S(2)}) collective-permute-start(bf16[288,768]{1,0:T(8,128)(2,1)S(1)} %collective-permute-done.5.refs_7_), channel_id=1, source_target_pairs={{0,32},{32,64},{64,96},{96,128},{128,160},{160,192},{192,224},{224... | collective-permute-start | bytes 1327112 | tf_op jit(solution)/shard_map/ppermute | solution.py:39
  47.8 13.3 %collective-permute-start.8 = (bf16[288,768]{1,0:T(8,128)(2,1)S(1)}, bf16[288,768]{1,0:T(8,128)(2,1)S(1)}, u32[]{:S(2)}, u32[]{:S(2)}) collective-permute-start(bf16[288,768]{1,0:T(8,128)(2,1)S(1)} %collective-permute-done.6.refs_8_), channel_id=1, source_target_pairs={{0,224},{32,0},{64,32},{96,64},{128,96},{160,128},{192,160},{224,1... | collective-permute-start | bytes 1327112 | tf_op jit(solution)/shard_map/ppermute | solution.py:39
  51.0 1.3 collective-permute-start.9
  61.1 14.1 %copy-start.5 = (bf16[288,768]{1,0:T(8,128)(2,1)}, bf16[288,768]{1,0:T(8,128)(2,1)S(1)}, u32[]{:S(2)}) copy-start(bf16[288,768]{1,0:T(8,128)(2,1)S(1)} %collective-permute-done.7.refs_9_) | copy-start | bytes 1327108
  61.1 12.6 %collective-permute-start.10 = (bf16[288,768]{1,0:T(8,128)(2,1)S(1)}, bf16[288,768]{1,0:T(8,128)(2,1)S(1)}, u32[]{:S(2)}, u32[]{:S(2)}) collective-permute-start(bf16[288,768]{1,0:T(8,128)(2,1)S(1)} %collective-permute-done.7.refs_9_), channel_id=1, source_target_pairs={{0,32},{32,64},{64,96},{96,128},{128,160},{160,192},{192,224},{224... | collective-permute-start | bytes 1327112 | tf_op jit(solution)/shard_map/ppermute | solution.py:39
  61.2 12.5 %collective-permute-start.11 = (bf16[288,768]{1,0:T(8,128)(2,1)S(1)}, bf16[288,768]{1,0:T(8,128)(2,1)S(1)}, u32[]{:S(2)}, u32[]{:S(2)}) collective-permute-start(bf16[288,768]{1,0:T(8,128)(2,1)S(1)} %collective-permute-done.8.refs_10_), channel_id=1, source_target_pairs={{0,224},{32,0},{64,32},{96,64},{128,96},{160,128},{192,160},{224,1... | collective-permute-start | bytes 1327112 | tf_op jit(solution)/shard_map/ppermute | solution.py:39
  64.4 0.8 copy-start.7
  65.3 5.4 %collective-permute-start.12 = (f32[2,3,768]{2,1,0:T(4,128)S(1)}, f32[2,3,768]{2,1,0:T(4,128)S(1)}, u32[]{:S(2)}, u32[]{:S(2)}) collective-permute-start(f32[2,3,768]{2,1,0:T(4,128)S(1)} %pad_maximum_fusion.4.refs_2_), channel_id=1, source_target_pairs={{0,16},{2,18},{16,0},{18,2},{1,17},{3,19},{17,1},{19,3},{4,20},{6,... | collective-permute-start | bytes 55304 | tf_op jit(solution)/shard_map/ppermute | solution.py:227
  66.5 4.2 %collective-permute-start.13 = (f32[2,3,768]{2,1,0:T(4,128)S(1)}, f32[2,3,768]{2,1,0:T(4,128)S(1)}, u32[]{:S(2)}, u32[]{:S(2)}) collective-permute-start(f32[2,3,768]{2,1,0:T(4,128)S(1)} %pad_maximum_fusion.4.refs_2_), channel_id=1, source_target_pairs={{0,2},{2,0},{16,18},{18,16},{1,3},{3,1},{17,19},{19,17},{4,6},{6,4... | collective-permute-start | bytes 55304 | tf_op jit(solution)/shard_map/ppermute | solution.py:227
  66.9 5.0 %collective-permute-start.14 = (f32[2,3,768]{2,1,0:T(4,128)S(1)}, f32[2,3,768]{2,1,0:T(4,128)S(1)}, u32[]{:S(2)}, u32[]{:S(2)}) collective-permute-start(f32[2,3,768]{2,1,0:T(4,128)S(1)} %pad_maximum_fusion.4.refs_2_), channel_id=1, source_target_pairs={{0,18},{2,16},{16,2},{18,0},{1,19},{3,17},{17,3},{19,1},{4,22},{6,... | collective-permute-start | bytes 55304 | tf_op jit(solution)/shard_map/ppermute | solution.py:227
  74.5 15.6 %collective-permute-start.15 = (bf16[144,768]{1,0:T(8,128)(2,1)}, bf16[144,768]{1,0:T(8,128)(2,1)}, u32[]{:S(2)}, u32[]{:S(2)}) collective-permute-start(bf16[144,768]{1,0:T(8,128)(2,1)} %slice.54), channel_id=1, source_target_pairs={{0,32},{32,64},{64,96},{96,128},{128,160},{160,192},{192,224},{224... | collective-permute-start | bytes 663560 | tf_op jit(solution)/shard_map/ppermute | solution.py:39
  75.2 14.9 %collective-permute-start.16 = (bf16[144,768]{1,0:T(8,128)(2,1)}, bf16[144,768]{1,0:T(8,128)(2,1)}, u32[]{:S(2)}, u32[]{:S(2)}) collective-permute-start(bf16[144,768]{1,0:T(8,128)(2,1)} %slice.55), channel_id=1, source_target_pairs={{0,224},{32,0},{64,32},{96,64},{128,96},{160,128},{192,160},{224,1... | collective-permute-start | bytes 663560 | tf_op jit(solution)/shard_map/ppermute | solution.py:39
  79.9 2.3 %copy-start = (bf16[3072,768]{1,0:T(8,128)(2,1)S(1)}, bf16[3072,768]{1,0:T(8,128)(2,1)}, u32[]{:S(2)}) copy-start(bf16[3072,768]{1,0:T(8,128)(2,1)} %all-gather.3.cloned.1.call-done) | copy-start | bytes 14155780
  82.3 1.0 copy-start.2
  83.3 1.0 copy-start.4
  84.3 1.0 copy-start.6
  85.3 1.0 copy-start.8
  93.8 1.3 collective-permute-start.17
  95.1 5.3 %collective-permute-start.18 = (f32[8,768]{1,0:T(8,128)S(1)}, f32[8,768]{1,0:T(8,128)S(1)}, u32[]{:S(2)}, u32[]{:S(2)}) collective-permute-start(f32[8,768]{1,0:T(8,128)S(1)} %add.112.refs_5_), channel_id=1, source_target_pairs={{0,16},{2,18},{16,0},{18,2},{1,17},{3,19},{17,1},{19,3},{4,20},{6,... | collective-permute-start | bytes 73736 | tf_op jit(solution)/shard_map/ppermute | solution.py:227
  95.9 5.0 %collective-permute-start.20 = (f32[8,768]{1,0:T(8,128)S(1)}, f32[8,768]{1,0:T(8,128)S(1)}, u32[]{:S(2)}, u32[]{:S(2)}) collective-permute-start(f32[8,768]{1,0:T(8,128)S(1)} %add.112.refs_5_), channel_id=1, source_target_pairs={{0,18},{2,16},{16,2},{18,0},{1,19},{3,17},{17,3},{19,1},{4,22},{6,... | collective-permute-start | bytes 73736 | tf_op jit(solution)/shard_map/ppermute | solution.py:227
  98.9 3.8 %collective-permute-start.19 = (f32[8,768]{1,0:T(8,128)S(1)}, f32[8,768]{1,0:T(8,128)S(1)}, u32[]{:S(2)}, u32[]{:S(2)}) collective-permute-start(f32[8,768]{1,0:T(8,128)S(1)} %add.112.refs_5_), channel_id=1, source_target_pairs={{0,2},{2,0},{16,18},{18,16},{1,3},{3,1},{17,19},{19,17},{4,6},{6,4... | collective-permute-start | bytes 73736 | tf_op jit(solution)/shard_map/ppermute | solution.py:227
  106.3 7.2 %collective-permute-start.21 = (bf16[144,768]{1,0:T(8,128)(2,1)S(1)}, bf16[144,768]{1,0:T(8,128)(2,1)S(1)}, u32[]{:S(2)}, u32[]{:S(2)}) collective-permute-start(bf16[144,768]{1,0:T(8,128)(2,1)S(1)} %get-tuple-element.66), channel_id=1, source_target_pairs={{0,32},{32,64},{64,96},{96,128},{128,160},{160,192},{192,224},{224... | collective-permute-start | bytes 663560 | tf_op jit(solution)/shard_map/ppermute | solution.py:39
  106.4 7.3 %collective-permute-start.25 = (bf16[144,768]{1,0:T(8,128)(2,1)S(1)}, bf16[144,768]{1,0:T(8,128)(2,1)S(1)}, u32[]{:S(2)}, u32[]{:S(2)}) collective-permute-start(bf16[144,768]{1,0:T(8,128)(2,1)S(1)} %get-tuple-element.74), channel_id=1, source_target_pairs={{0,224},{32,0},{64,32},{96,64},{128,96},{160,128},{192,160},{224,1... | collective-permute-start | bytes 663560 | tf_op jit(solution)/shard_map/ppermute | solution.py:39
  113.6 10.7 %collective-permute-start.22 = (bf16[288,768]{1,0:T(8,128)(2,1)S(1)}, bf16[288,768]{1,0:T(8,128)(2,1)S(1)}, u32[]{:S(2)}, u32[]{:S(2)}) collective-permute-start(bf16[288,768]{1,0:T(8,128)(2,1)S(1)} %pad_maximum_fusion.2), channel_id=1, source_target_pairs={{0,32},{32,64},{64,96},{96,128},{128,160},{160,192},{192,224},{224... | collective-permute-start | bytes 1327112 | tf_op jit(solution)/shard_map/ppermute | solution.py:39
  113.8 10.7 %collective-permute-start.26 = (bf16[288,768]{1,0:T(8,128)(2,1)S(1)}, bf16[288,768]{1,0:T(8,128)(2,1)S(1)}, u32[]{:S(2)}, u32[]{:S(2)}) collective-permute-start(bf16[288,768]{1,0:T(8,128)(2,1)S(1)} %pad_maximum_fusion.3), channel_id=1, source_target_pairs={{0,224},{32,0},{64,32},{96,64},{128,96},{160,128},{192,160},{224,1... | collective-permute-start | bytes 1327112 | tf_op jit(solution)/shard_map/ppermute | solution.py:39
  124.4 10.2 %collective-permute-start.23 = (bf16[288,768]{1,0:T(8,128)(2,1)S(1)}, bf16[288,768]{1,0:T(8,128)(2,1)S(1)}, u32[]{:S(2)}, u32[]{:S(2)}) collective-permute-start(bf16[288,768]{1,0:T(8,128)(2,1)S(1)} %add_convert_fusion.3), channel_id=1, source_target_pairs={{0,32},{32,64},{64,96},{96,128},{128,160},{160,192},{192,224},{224... | collective-permute-start | bytes 1327112 | tf_op jit(solution)/shard_map/ppermute | solution.py:39
  124.6 10.2 %collective-permute-start.27 = (bf16[288,768]{1,0:T(8,128)(2,1)S(1)}, bf16[288,768]{1,0:T(8,128)(2,1)S(1)}, u32[]{:S(2)}, u32[]{:S(2)}) collective-permute-start(bf16[288,768]{1,0:T(8,128)(2,1)S(1)} %add_convert_fusion.1), channel_id=1, source_target_pairs={{0,224},{32,0},{64,32},{96,64},{128,96},{160,128},{192,160},{224,1... | collective-permute-start | bytes 1327112 | tf_op jit(solution)/shard_map/ppermute | solution.py:39
  128.1 10.1 %collective-permute-start.33 = (bf16[2,4,72,384]{3,2,1,0:T(8,128)(2,1)S(1)}, bf16[2,4,72,384]{3,2,1,0:T(8,128)(2,1)}, u32[]{:S(2)}, u32[]{:S(2)}) collective-permute-start(bf16[2,4,72,384]{3,2,1,0:T(8,128)(2,1)S(1)} %slice.81), channel_id=1, source_target_pairs={{0,16},{16,0},{1,17},{17,1},{2,18},{18,2},{3,19},{19,3},{4,20},{20... | collective-permute-start | bytes 1327112 | tf_op jit(solution)/shard_map/ppermute | solution.py:39
  134.7 9.6 %collective-permute-start.24 = (bf16[288,768]{1,0:T(8,128)(2,1)S(1)}, bf16[288,768]{1,0:T(8,128)(2,1)S(1)}, u32[]{:S(2)}, u32[]{:S(2)}) collective-permute-start(bf16[288,768]{1,0:T(8,128)(2,1)S(1)} %add_convert_fusion.2), channel_id=1, source_target_pairs={{0,32},{32,64},{64,96},{96,128},{128,160},{160,192},{192,224},{224... | collective-permute-start | bytes 1327112 | tf_op jit(solution)/shard_map/ppermute | solution.py:39
  134.9 9.4 %collective-permute-start.28 = (bf16[288,768]{1,0:T(8,128)(2,1)S(1)}, bf16[288,768]{1,0:T(8,128)(2,1)}, u32[]{:S(2)}, u32[]{:S(2)}) collective-permute-start(bf16[288,768]{1,0:T(8,128)(2,1)S(1)} %add_convert_fusion), channel_id=1, source_target_pairs={{0,224},{32,0},{64,32},{96,64},{128,96},{160,128},{192,160},{224,1... | collective-permute-start | bytes 1327112 | tf_op jit(solution)/shard_map/ppermute | solution.py:39
  145.5 5.7 %collective-permute-start.29 = (bf16[72,768]{1,0:T(8,128)(2,1)S(1)}, bf16[72,768]{1,0:T(8,128)(2,1)S(1)}, u32[]{:S(2)}, u32[]{:S(2)}) collective-permute-start(bf16[72,768]{1,0:T(8,128)(2,1)S(1)} %get-tuple-element.94), channel_id=1, source_target_pairs={{0,12},{4,0},{8,4},{12,8},{1,13},{5,1},{9,5},{13,9},{2,14},{6,2},{... | collective-permute-start | bytes 331784 | tf_op jit(solution)/shard_map/ppermute | solution.py:39
  148.6 6.3 %collective-permute-start.30 = (bf16[72,768]{1,0:T(8,128)(2,1)S(1)}, bf16[72,768]{1,0:T(8,128)(2,1)S(1)}, u32[]{:S(2)}, u32[]{:S(2)}) collective-permute-start(bf16[72,768]{1,0:T(8,128)(2,1)S(1)} %get-tuple-element.96), channel_id=1, source_target_pairs={{0,8},{4,12},{8,0},{12,4},{1,9},{5,13},{9,1},{13,5},{2,10},{6,14},... | collective-permute-start | bytes 331784 | tf_op jit(solution)/shard_map/ppermute | solution.py:39
  149.2 6.8 %collective-permute-start.31 = (bf16[72,768]{1,0:T(8,128)(2,1)S(1)}, bf16[72,768]{1,0:T(8,128)(2,1)S(1)}, u32[]{:S(2)}, u32[]{:S(2)}) collective-permute-start(bf16[72,768]{1,0:T(8,128)(2,1)S(1)} %get-tuple-element.95), channel_id=1, source_target_pairs={{0,4},{4,8},{8,12},{12,0},{1,5},{5,9},{9,13},{13,1},{2,6},{6,10},{... | collective-permute-start | bytes 331784 | tf_op jit(solution)/shard_map/ppermute | solution.py:39
  156.1 11.4 %collective-permute-start.32 = (bf16[72,768]{1,0:T(8,128)(2,1)S(1)}, bf16[72,768]{1,0:T(8,128)(2,1)S(1)}, u32[]{:S(2)}, u32[]{:S(2)}) collective-permute-start(bf16[72,768]{1,0:T(8,128)(2,1)S(1)} %fusion), channel_id=1, source_target_pairs={{0,0},{64,1},{128,2},{192,3},{4,4},{68,5},{132,6},{196,7},{8,8},{7... | collective-permute-start | bytes 331784 | tf_op jit(solution)/shard_map/ppermute | solution.py:349
Sparse Core Ops, SparseCore 0:
  33.0 36.5 all-gather.2
where the time goes:
time: 176 us; the launch traced here: 175 us
  waiting for transfers between devices  63.9 us (36%)
  starting transfers between devices  61 us (35%)
  between operations  14.7 us (8%)
  local copies, waits for them, and re-layouts  14.6 us (8%)
  Pallas kernels  14.5 us (8%)
  other arithmetic  6.43 us (4%)
    ppermute x24, waiting for transfers between devices, shift(): return lax.ppermute(x, axis, [(i, (i + by) % n) for i in range(n)])  48.7 us
    ppermute x24, starting transfers between devices, shift(): return lax.ppermute(x, axis, [(i, (i + by) % n) for i in range(n)])  39.6 us
    pallas_call x4, Pallas kernels, call(): pl.pallas_call(body, out_shape=outs, in_specs=[pl.BlockSpec(memory_space=...  14.5 us
    ppermute x1, starting transfers between devices, on_device(): block = lax.ppermute(tangent, ALL, THERE)  9.36 us
    ppermute x8, waiting for transfers between devices, flip(): return lax.ppermute(x, axes, [(i, i ^ by) for i in range(n)])  8.34 us
    ppermute x8, starting transfers between devices, flip(): return lax.ppermute(x, axes, [(i, i ^ by) for i in range(n)])  8.15 us
    unnamed x38, local copies, waits for them, and re-layouts  7.28 us
    ppermute x1, waiting for transfers between devices, on_device(): product = lax.ppermute(product.astype(bf16), ALL, BACK).astype(f32)  6.29 us
  transfers between devices with their start and end apart: 35, of which 20 were waited for; matrix products, arithmetic and copies ran while one was open for 7% of the time, Pallas kernels for 4%

commit v1 on v0

--- a/solution.py
+++ b/solution.py
@@ -93,8 +93,6 @@
 def add_pieces(offsets, place, heads, pieces, halves):
     for i, offset in enumerate(offsets):
         piece = pieces[i][...]
-        if offset == 4:
-            piece = jnp.concatenate([piece, pieces[i + 1][...]], axis=0)
         term = lax.dot_general(
             piece,
             heads[group(place, offset)],
@@ -260,7 +258,7 @@
     (beside,) = step(flip(stats, "c", 1))
     stats = jnp.stack([stats, beside])
     x2, x1, x3 = step(*(flip(stats, XRING, by) for by in (2, 1, 3)))
-    across = [shift(up[3][:middle], "z", 1), shift(down[3][middle:], "z", -1)]
+    across = [shift(up[3], "z", 1)]
     (gathered,) = after(up[2], gathered)
     place = jnp.stack([z, 2 * l + c, h]).astype(jnp.int32)
     shape = (2, quarter, 2 * rows)

time: 176 us -> 172 us (0.977)
  starting transfers between devices: 61 us -> 57.9 us
  waiting for transfers between devices: 63.9 us -> 66 us
  local copies, waits for them, and re-layouts: 14.6 us -> 12.6 us
    ppermute x24 -> x23, starting transfers between devices: 39.6 us -> 36.3 us  [shift(): return lax.ppermute(x, axis, [(i, (i + by) % n) for i in range(n)])]
    ppermute x24 -> x23, waiting for transfers between devices: 48.7 us -> 50.5 us  [shift(): return lax.ppermute(x, axis, [(i, (i + by) % n) for i in range(n)])]
    unnamed x38 -> x34, local copies, waits for them, and re-layouts: 7.28 us -> 6.78 us
  transfers between devices with their start and end apart: 35 -> 34, of which waited for: 20 -> 21; matrix products, arithmetic and copies ran while one was open for 7% -> 6% of each run, Pallas kernels for 4% -> 4%
where the time goes in v1:
time: 172 us
  waiting for transfers between devices  66 us (38%)
  starting transfers between devices  57.9 us (34%)
  Pallas kernels  14.6 us (8%)
  between operations  14.6 us (8%)
  local copies, waits for them, and re-layouts  12.6 us (7%)
  other arithmetic  6.34 us (4%)
    ppermute x23, waiting for transfers between devices, shift(): return lax.ppermute(x, axis, [(i, (i + by) % n) for i in range(n)])  50.5 us
    ppermute x23, starting transfers between devices, shift(): return lax.ppermute(x, axis, [(i, (i + by) % n) for i in range(n)])  36.3 us
    pallas_call x4, Pallas kernels, call(): pl.pallas_call(body, out_shape=outs, in_specs=[pl.BlockSpec(memory_space=...  14.6 us
    ppermute x1, starting transfers between devices, on_device(): block = lax.ppermute(tangent, ALL, THERE)  9.36 us
    ppermute x8, waiting for transfers between devices, flip(): return lax.ppermute(x, axes, [(i, i ^ by) for i in range(n)])  8.57 us
    ppermute x8, starting transfers between devices, flip(): return lax.ppermute(x, axes, [(i, i ^ by) for i in range(n)])  8.4 us
    unnamed x34, local copies, waits for them, and re-layouts  6.78 us
    ppermute x1, waiting for transfers between devices, on_device(): product = lax.ppermute(product.astype(bf16), ALL, BACK).astype(f32)  6.38 us
  transfers between devices with their start and end apart: 34, of which 21 were waited for; matrix products, arithmetic and copies ran while one was open for 6% of the time, Pallas kernels for 4%

profile of v1, /device:TPU:6, one launch (start us, length us, event | category | flops | bytes accessed | tf_op | source)
XLA Modules:
  0.0 172.0 jit_solution(14272166031346954115)
XLA Ops:
  7.2 9.4 %collective-permute-start = (bf16[72,768]{1,0:T(8,128)(2,1)}, bf16[72,768]{1,0:T(8,128)(2,1)S(1)}, u32[]{:S(2)}, u32[]{:S(2)}) collective-permute-start(bf16[72,768]{1,0:T(8,128)(2,1)} %param.8), channel_id=1, source_target_pairs={{0,0},{1,64},{2,128},{3,192},{4,4},{5,68},{6,132},{7,196},{8,8},{9... | collective-permute-start | bytes 331784 | tf_op jit(solution)/shard_map/ppermute | solution.py:214
  16.6 1.2 slice.59
  17.8 0.9 copy.22
  18.9 0.5 collective-permute-done
  19.4 1.4 collective-permute-start.4
  20.7 1.6 collective-permute-start.1
  22.3 2.9 %collective-permute-start.2 = (bf16[72,768]{1,0:T(8,128)(2,1)S(1)}, bf16[72,768]{1,0:T(8,128)(2,1)S(1)}, u32[]{:S(2)}, u32[]{:S(2)}) collective-permute-start(bf16[72,768]{1,0:T(8,128)(2,1)S(1)} %collective-permute-done), channel_id=1, source_target_pairs={{0,8},{4,12},{8,0},{12,4},{1,9},{5,13},{9,1},{13,5},{2,10},{6,14},... | collective-permute-start | bytes 331784 | tf_op jit(solution)/shard_map/ppermute | solution.py:39
  25.2 1.3 collective-permute-start.3
  26.6 0.9 slice.62
  27.4 3.6 %collective-permute-done.2 = bf16[72,768]{1,0:T(8,128)(2,1)S(1)} collective-permute-done((bf16[72,768]{1,0:T(8,128)(2,1)S(1)}, bf16[72,768]{1,0:T(8,128)(2,1)S(1)}, u32[]{:S(2)}, u32[]{:S(2)}) %collective-permute-start.2) | collective-permute-done | bytes 110624 | tf_op jit(solution)/shard_map/ppermute | solution.py:39
  31.1 1.8 %collective-permute-done.4 = bf16[2,4,72,384]{3,2,1,0:T(8,128)(2,1)S(1)} collective-permute-done((bf16[2,4,72,384]{3,2,1,0:T(8,128)(2,1)S(1)}, bf16[2,4,72,384]{3,2,1,0:T(8,128)(2,1)S(1)}, u32[]{:S(2)}, u32[]{:S(2)}) %collective-permute-start.4) | collective-permute-done | bytes 442400 | tf_op jit(solution)/shard_map/ppermute | solution.py:39
  33.4 1.6 collective-permute-start.5
  35.1 1.7 collective-permute-start.6
  37.3 0.3 multiply_reduce_fusion
  37.6 10.1 %collective-permute-done.5.refs_7_ = bf16[288,768]{1,0:T(8,128)(2,1)S(1)} collective-permute-done((bf16[288,768]{1,0:T(8,128)(2,1)S(1)}, bf16[288,768]{1,0:T(8,128)(2,1)S(1)}, u32[]{:S(2)}, u32[]{:S(2)}) %collective-permute-start.5) | collective-permute-done | bytes 442400 | tf_op jit(solution)/shard_map/ppermute | solution.py:39
  47.7 3.2 %collective-permute-start.8 = (bf16[288,768]{1,0:T(8,128)(2,1)S(1)}, bf16[288,768]{1,0:T(8,128)(2,1)S(1)}, u32[]{:S(2)}, u32[]{:S(2)}) collective-permute-start(bf16[288,768]{1,0:T(8,128)(2,1)S(1)} %collective-permute-done.6.refs_8_), channel_id=1, source_target_pairs={{0,224},{32,0},{64,32},{96,64},{128,96},{160,128},{192,160},{224,1... | collective-permute-start | bytes 1327112 | tf_op jit(solution)/shard_map/ppermute | solution.py:39
  51.1 1.1 collective-permute-done.9
  52.2 8.8 %collective-permute-done.7.refs_9_ = bf16[288,768]{1,0:T(8,128)(2,1)S(1)} collective-permute-done((bf16[288,768]{1,0:T(8,128)(2,1)S(1)}, bf16[288,768]{1,0:T(8,128)(2,1)S(1)}, u32[]{:S(2)}, u32[]{:S(2)}) %collective-permute-start.7) | collective-permute-done | bytes 442400 | tf_op jit(solution)/shard_map/ppermute | solution.py:39
  61.0 0.8 copy-done.1
  61.7 3.2 %collective-permute-start.11 = (bf16[288,768]{1,0:T(8,128)(2,1)S(1)}, bf16[288,768]{1,0:T(8,128)(2,1)S(1)}, u32[]{:S(2)}, u32[]{:S(2)}) collective-permute-start(bf16[288,768]{1,0:T(8,128)(2,1)S(1)} %collective-permute-done.8.refs_10_), channel_id=1, source_target_pairs={{0,224},{32,0},{64,32},{96,64},{128,96},{160,128},{192,160},{224,1... | collective-permute-start | bytes 1327112 | tf_op jit(solution)/shard_map/ppermute | solution.py:39
  65.0 0.8 copy-done.3
  65.8 1.2 collective-permute-start.12
  67.0 0.3 collective-permute-start.13
  67.4 2.6 %collective-permute-start.14 = (f32[2,3,768]{2,1,0:T(4,128)S(1)}, f32[2,3,768]{2,1,0:T(4,128)S(1)}, u32[]{:S(2)}, u32[]{:S(2)}) collective-permute-start(f32[2,3,768]{2,1,0:T(4,128)S(1)} %pad_maximum_fusion.4.refs_2_), channel_id=1, source_target_pairs={{0,18},{2,16},{16,2},{18,0},{1,19},{3,17},{17,3},{19,1},{4,22},{6,... | collective-permute-start | bytes 55304 | tf_op jit(solution)/shard_map/ppermute | solution.py:225
  70.0 1.2 collective-permute-done.12.refs_3_
  71.2 1.2 collective-permute-done.14.refs_5_
  72.4 1.2 collective-permute-done.10.refs_4_
  73.6 0.8 copy-done.5
  74.8 1.4 maximum_convert_fusion.refs_1_
  76.2 2.3 %copy-done = bf16[3072,768]{1,0:T(8,128)(2,1)S(1)} copy-done((bf16[3072,768]{1,0:T(8,128)(2,1)S(1)}, bf16[3072,768]{1,0:T(8,128)(2,1)}, u32[]{:S(2)}) %copy-start) | copy-done | bytes 4718616
  78.5 1.0 copy-done.2
  79.5 1.0 copy-done.4
  80.5 3.7 %shard_map.77 = (f32[2,288,768]{2,1,0:T(8,128)S(1)}, f32[2,288,768]{2,1,0:T(8,128)S(1)}, f32[2,768]{1,0:T(2,128)S(1)}) custom-call(s32[3]{0:T(128)S(1)} %pad_add_fusion.place_ref, bf16[8,384,768]{2,1,0:T(8,128)(2,1)S(1)} %bitcast.45, f32[2,288,768]{2,1,0:T(8,128)S(1)} %maximum_convert_fusion.refs_1_, f32[2,3,768]{2,1,0:T(4,128)S(1)} %pad_maximum_fusion.4.refs_2_, ...), custom_call_target="tpu_custom_call" | custom-call | flops 1698693120 | bytes 12318720 | tf_op jit(solution)/shard_map/pallas_call | solution.py:66
  84.3 2.4 %collective-permute-done.15.refs_6_ = bf16[288,768]{1,0:T(8,128)(2,1)} collective-permute-done((bf16[288,768]{1,0:T(8,128)(2,1)}, bf16[288,768]{1,0:T(8,128)(2,1)}, u32[]{:S(2)}, u32[]{:S(2)}) %collective-permute-start.15) | collective-permute-done | bytes 442400 | tf_op jit(solution)/shard_map/ppermute | solution.py:39
  86.7 3.8 %shard_map.78 = (f32[2,288,768]{2,1,0:T(8,128)S(1)}, f32[8,768]{1,0:T(8,128)S(1)}) custom-call(s32[3]{0:T(128)S(1)} %pad_add_fusion.place_ref, bf16[8,384,768]{2,1,0:T(8,128)(2,1)S(1)} %bitcast.46, f32[2,288,768]{2,1,0:T(8,128)S(1)} %get-tuple-element.59.refs_1_, f32[2,288,768]{2,1,0:T(8,128)S(1)} %get-tuple-element.60.refs_2_, ...), custom_call_target="tpu_custom_call" | custom-call | flops 1019215872 | bytes 11380992 | tf_op jit(solution)/shard_map/pallas_call | solution.py:66
  90.6 1.2 collective-permute-done.16
  91.8 0.5 collective-permute-start.17
  92.3 3.5 %collective-permute-start.19 = (f32[8,768]{1,0:T(8,128)S(1)}, f32[8,768]{1,0:T(8,128)S(1)}, u32[]{:S(2)}, u32[]{:S(2)}) collective-permute-start(f32[8,768]{1,0:T(8,128)S(1)} %add.112.refs_5_), channel_id=1, source_target_pairs={{0,18},{2,16},{16,2},{18,0},{1,19},{3,17},{17,3},{19,1},{4,22},{6,... | collective-permute-start | bytes 73736 | tf_op jit(solution)/shard_map/ppermute | solution.py:225
  95.8 1.3 collective-permute-done.17
  97.1 0.5 collective-permute-done.19
  97.7 2.0 %collective-permute-done.18.refs_7_ = f32[8,768]{1,0:T(8,128)S(1)} collective-permute-done((f32[8,768]{1,0:T(8,128)S(1)}, f32[8,768]{1,0:T(8,128)S(1)}, u32[]{:S(2)}, u32[]{:S(2)}) %collective-permute-start.18) | collective-permute-done | bytes 24608 | tf_op jit(solution)/shard_map/ppermute | solution.py:225
  99.7 3.6 %shard_map.79 = (bf16[2,288,768]{2,1,0:T(8,128)(2,1)S(1)}, bf16[2,288,768]{2,1,0:T(8,128)(2,1)S(1)}, bf16[144,768]{1,0:T(8,128)(2,1)S(1)}, bf16[144,768]{1,0:T(8...) custom-call(s32[3]{0:T(128)S(1)} %pad_add_fusion.place_ref, ...), custom_call_target="tpu_custom_call" | custom-call | flops 1019215872 | bytes 12345600 | tf_op jit(solution)/shard_map/pallas_call | solution.py:66
  103.4 3.3 %collective-permute-start.24 = (bf16[144,768]{1,0:T(8,128)(2,1)S(1)}, bf16[144,768]{1,0:T(8,128)(2,1)S(1)}, u32[]{:S(2)}, u32[]{:S(2)}) collective-permute-start(bf16[144,768]{1,0:T(8,128)(2,1)S(1)} %get-tuple-element.74), channel_id=1, source_target_pairs={{0,224},{32,0},{64,32},{96,64},{128,96},{160,128},{192,160},{224,1... | collective-permute-start | bytes 663560 | tf_op jit(solution)/shard_map/ppermute | solution.py:39
  106.8 3.7 %collective-permute-done.20 = bf16[144,768]{1,0:T(8,128)(2,1)S(1)} collective-permute-done((bf16[144,768]{1,0:T(8,128)(2,1)S(1)}, bf16[144,768]{1,0:T(8,128)(2,1)S(1)}, u32[]{:S(2)}, u32[]{:S(2)}) %collective-permute-start.20) | collective-permute-done | bytes 221216 | tf_op jit(solution)/shard_map/ppermute | solution.py:39
  110.7 3.5 %collective-permute-start.25 = (bf16[288,768]{1,0:T(8,128)(2,1)S(1)}, bf16[288,768]{1,0:T(8,128)(2,1)S(1)}, u32[]{:S(2)}, u32[]{:S(2)}) collective-permute-start(bf16[288,768]{1,0:T(8,128)(2,1)S(1)} %pad_maximum_fusion.3), channel_id=1, source_target_pairs={{0,224},{32,0},{64,32},{96,64},{128,96},{160,128},{192,160},{224,1... | collective-permute-start | bytes 1327112 | tf_op jit(solution)/shard_map/ppermute | solution.py:39
  114.4 3.5 %shard_map.80 = (f32[288,768]{1,0:T(8,128)S(1)}, f32[288,768]{1,0:T(8,128)S(1)}, f32[288,768]{1,0:T(8,128)S(1)}, f32[288,768]{1,0:T(8,128)S(1)}, f32[288,768]{1,0:T(8,128)S(1)}) custom-call(s32[3]{0:T(128)S(1)} %pad_add_fusion.place_ref, bf16[8,384,768]{2,1,0:T(8,128)(2,1)S(1)} %bitcast.48, bf16[2,288,768]{2,1,0:T(8,128)(2,1)S(1)} %get-tuple-element.70.refs_1_), custom_call_target="tpu_custom_call" | custom-call | flops 1698693120 | bytes 10027008 | tf_op jit(solution)/shard_map/pallas_call | solution.py:66
  117.9 3.4 %collective-permute-done.21 = bf16[288,768]{1,0:T(8,128)(2,1)S(1)} collective-permute-done((bf16[288,768]{1,0:T(8,128)(2,1)S(1)}, bf16[288,768]{1,0:T(8,128)(2,1)S(1)}, u32[]{:S(2)}, u32[]{:S(2)}) %collective-permute-start.21) | collective-permute-done | bytes 442400 | tf_op jit(solution)/shard_map/ppermute | solution.py:39
  121.5 3.3 %collective-permute-start.26 = (bf16[288,768]{1,0:T(8,128)(2,1)S(1)}, bf16[288,768]{1,0:T(8,128)(2,1)S(1)}, u32[]{:S(2)}, u32[]{:S(2)}) collective-permute-start(bf16[288,768]{1,0:T(8,128)(2,1)S(1)} %add_convert_fusion.1), channel_id=1, source_target_pairs={{0,224},{32,0},{64,32},{96,64},{128,96},{160,128},{192,160},{224,1... | collective-permute-start | bytes 1327112 | tf_op jit(solution)/shard_map/ppermute | solution.py:39
  125.0 0.9 collective-permute-start.32
  125.9 5.7 %collective-permute-done.22 = bf16[288,768]{1,0:T(8,128)(2,1)S(1)} collective-permute-done((bf16[288,768]{1,0:T(8,128)(2,1)S(1)}, bf16[288,768]{1,0:T(8,128)(2,1)S(1)}, u32[]{:S(2)}, u32[]{:S(2)}) %collective-permute-start.22) | collective-permute-done | bytes 442400 | tf_op jit(solution)/shard_map/ppermute | solution.py:39
  131.8 3.3 %collective-permute-start.27 = (bf16[288,768]{1,0:T(8,128)(2,1)S(1)}, bf16[288,768]{1,0:T(8,128)(2,1)}, u32[]{:S(2)}, u32[]{:S(2)}) collective-permute-start(bf16[288,768]{1,0:T(8,128)(2,1)S(1)} %add_convert_fusion), channel_id=1, source_target_pairs={{0,224},{32,0},{64,32},{96,64},{128,96},{160,128},{192,160},{224,1... | collective-permute-start | bytes 1327112 | tf_op jit(solution)/shard_map/ppermute | solution.py:39
  135.1 1.1 select_bitcast_fusion.1
  136.2 5.0 %collective-permute-done.23 = bf16[288,768]{1,0:T(8,128)(2,1)S(1)} collective-permute-done((bf16[288,768]{1,0:T(8,128)(2,1)S(1)}, bf16[288,768]{1,0:T(8,128)(2,1)S(1)}, u32[]{:S(2)}, u32[]{:S(2)}) %collective-permute-start.23) | collective-permute-done | bytes 442400 | tf_op jit(solution)/shard_map/ppermute | solution.py:39
  141.2 1.1 fusion.3
  142.4 3.1 %collective-permute-start.28 = (bf16[72,768]{1,0:T(8,128)(2,1)S(1)}, bf16[72,768]{1,0:T(8,128)(2,1)S(1)}, u32[]{:S(2)}, u32[]{:S(2)}) collective-permute-start(bf16[72,768]{1,0:T(8,128)(2,1)S(1)} %get-tuple-element.94), channel_id=1, source_target_pairs={{0,12},{4,0},{8,4},{12,8},{1,13},{5,1},{9,5},{13,9},{2,14},{6,2},{... | collective-permute-start | bytes 331784 | tf_op jit(solution)/shard_map/ppermute | solution.py:39
  145.5 0.6 collective-permute-start.29
  146.1 1.0 collective-permute-start.30
  147.2 0.9 copy.26
  148.1 3.7 %collective-permute-done.29 = bf16[72,768]{1,0:T(8,128)(2,1)S(1)} collective-permute-done((bf16[72,768]{1,0:T(8,128)(2,1)S(1)}, bf16[72,768]{1,0:T(8,128)(2,1)S(1)}, u32[]{:S(2)}, u32[]{:S(2)}) %collective-permute-start.29) | collective-permute-done | bytes 110624 | tf_op jit(solution)/shard_map/ppermute | solution.py:39
  151.9 1.1 collective-permute-done.30
  153.0 3.8 %collective-permute-start.31 = (bf16[72,768]{1,0:T(8,128)(2,1)S(1)}, bf16[72,768]{1,0:T(8,128)(2,1)S(1)}, u32[]{:S(2)}, u32[]{:S(2)}) collective-permute-start(bf16[72,768]{1,0:T(8,128)(2,1)S(1)} %fusion), channel_id=1, source_target_pairs={{0,0},{64,1},{128,2},{192,3},{4,4},{68,5},{132,6},{196,7},{8,8},{7... | collective-permute-start | bytes 331784 | tf_op jit(solution)/shard_map/ppermute | solution.py:347
  157.0 1.1 pad.4
  158.1 6.4 %collective-permute-done.31 = bf16[72,768]{1,0:T(8,128)(2,1)S(1)} collective-permute-done((bf16[72,768]{1,0:T(8,128)(2,1)S(1)}, bf16[72,768]{1,0:T(8,128)(2,1)S(1)}, u32[]{:S(2)}, u32[]{:S(2)}) %collective-permute-start.31) | collective-permute-done | bytes 110624 | tf_op jit(solution)/shard_map/ppermute | solution.py:347
  164.5 0.7 convert_element_type.88
  (100 shorter events, 3.5 us)
Async XLA Ops:
  7.2 69.0 %all-gather.3.cloned.1.call-start = ((), (), s32[]{:S(2)}) async-start(), calls=%async_computation | async-start | bytes 5308416 | tf_op jit(solution)/shard_map/all_gather | solution.py:221
  7.2 12.2 %collective-permute-start = (bf16[72,768]{1,0:T(8,128)(2,1)}, bf16[72,768]{1,0:T(8,128)(2,1)S(1)}, u32[]{:S(2)}, u32[]{:S(2)}) collective-permute-start(bf16[72,768]{1,0:T(8,128)(2,1)} %param.8), channel_id=1, source_target_pairs={{0,0},{1,64},{2,128},{3,192},{4,4},{5,68},{6,132},{7,196},{8,8},{9... | collective-permute-start | bytes 331784 | tf_op jit(solution)/shard_map/ppermute | solution.py:214
  17.8 8.7 %copy-start.11 = (bf16[512,768]{1,0:T(8,128)(2,1)S(1)}, bf16[512,768]{1,0:T(8,128)(2,1)}, u32[]{:S(2)}) copy-start(bf16[512,768]{1,0:T(8,128)(2,1)} %param.6) | copy-start | bytes 2359300
  18.7 14.3 %copy-start.13 = (f32[512]{0:T(512)S(1)}, f32[512]{0:T(512)}, u32[]{:S(2)}) copy-start(f32[512]{0:T(512)} %param.10) | copy-start | bytes 6148
  18.7 14.3 %copy-start.14 = (s32[2]{0:T(128)S(1)}, s32[2]{0:T(128)}, u32[]{:S(2)}) copy-start(s32[2]{0:T(128)} %param.11) | copy-start | bytes 28
  18.7 14.5 %copy-start.12 = (bf16[1152]{0:T(1024)(128)(2,1)S(1)}, bf16[1152]{0:T(1024)(128)(2,1)}, u32[]{:S(2)}) copy-start(bf16[1152]{0:T(1024)(128)(2,1)} %param.9) | copy-start | bytes 6916
  19.4 13.5 %collective-permute-start.4 = (bf16[2,4,72,384]{3,2,1,0:T(8,128)(2,1)S(1)}, bf16[2,4,72,384]{3,2,1,0:T(8,128)(2,1)S(1)}, u32[]{:S(2)}, u32[]{:S(2)}) collective-permute-start(bf16[2,4,72,384]{3,2,1,0:T(8,128)(2,1)S(1)} %get-tuple-element.42), channel_id=1, source_target_pairs={{0,16},{16,0},{1,17},{17,1},{2,18},{18,2},{3,19},{19,3},{4,20},{20... | collective-permute-start | bytes 1327112 | tf_op jit(solution)/shard_map/ppermute | solution.py:39
  20.7 6.7 %collective-permute-start.1 = (bf16[72,768]{1,0:T(8,128)(2,1)S(1)}, bf16[72,768]{1,0:T(8,128)(2,1)S(1)}, u32[]{:S(2)}, u32[]{:S(2)}) collective-permute-start(bf16[72,768]{1,0:T(8,128)(2,1)S(1)} %collective-permute-done), channel_id=1, source_target_pairs={{0,4},{4,8},{8,12},{12,0},{1,5},{5,9},{9,13},{13,1},{2,6},{6,10},{... | collective-permute-start | bytes 331784 | tf_op jit(solution)/shard_map/ppermute | solution.py:39
  22.3 8.7 %collective-permute-start.2 = (bf16[72,768]{1,0:T(8,128)(2,1)S(1)}, bf16[72,768]{1,0:T(8,128)(2,1)S(1)}, u32[]{:S(2)}, u32[]{:S(2)}) collective-permute-start(bf16[72,768]{1,0:T(8,128)(2,1)S(1)} %collective-permute-done), channel_id=1, source_target_pairs={{0,8},{4,12},{8,0},{12,4},{1,9},{5,13},{9,1},{13,5},{2,10},{6,14},... | collective-permute-start | bytes 331784 | tf_op jit(solution)/shard_map/ppermute | solution.py:39
  25.2 5.9 %collective-permute-start.3 = (bf16[72,768]{1,0:T(8,128)(2,1)S(1)}, bf16[72,768]{1,0:T(8,128)(2,1)S(1)}, u32[]{:S(2)}, u32[]{:S(2)}) collective-permute-start(bf16[72,768]{1,0:T(8,128)(2,1)S(1)} %collective-permute-done), channel_id=1, source_target_pairs={{0,12},{4,0},{8,4},{12,8},{1,13},{5,1},{9,5},{13,9},{2,14},{6,2},{... | collective-permute-start | bytes 331784 | tf_op jit(solution)/shard_map/ppermute | solution.py:39
  33.4 14.2 %collective-permute-start.5 = (bf16[288,768]{1,0:T(8,128)(2,1)S(1)}, bf16[288,768]{1,0:T(8,128)(2,1)S(1)}, u32[]{:S(2)}, u32[]{:S(2)}) collective-permute-start(bf16[288,768]{1,0:T(8,128)(2,1)S(1)} %constant_dynamic-update-slice_fusion.refs_6_), channel_id=1, source_target_pairs={{0,32},{32,64},{64,96},{96,128},{128,160},{160,192},{192,224},{224... | collective-permute-start | bytes 1327112 | tf_op jit(solution)/shard_map/ppermute | solution.py:39
  35.1 12.6 %collective-permute-start.6 = (bf16[288,768]{1,0:T(8,128)(2,1)S(1)}, bf16[288,768]{1,0:T(8,128)(2,1)S(1)}, u32[]{:S(2)}, u32[]{:S(2)}) collective-permute-start(bf16[288,768]{1,0:T(8,128)(2,1)S(1)} %constant_dynamic-update-slice_fusion.refs_6_), channel_id=1, source_target_pairs={{0,224},{32,0},{64,32},{96,64},{128,96},{160,128},{192,160},{224,1... | collective-permute-start | bytes 1327112 | tf_op jit(solution)/shard_map/ppermute | solution.py:39
  37.1 36.5 %copy-start.7 = (bf16[2,72,768]{2,1,0:T(8,128)(2,1)}, bf16[2,72,768]{2,1,0:T(8,128)(2,1)S(1)}, u32[]{:S(2)}) copy-start(bf16[2,72,768]{2,1,0:T(8,128)(2,1)S(1)} %get-tuple-element.88) | copy-start | bytes 663556
  37.1 37.3 %copy-start.8 = (bf16[2,72,768]{2,1,0:T(8,128)(2,1)}, bf16[2,72,768]{2,1,0:T(8,128)(2,1)S(1)}, u32[]{:S(2)}) copy-start(bf16[2,72,768]{2,1,0:T(8,128)(2,1)S(1)} %get-tuple-element.89) | copy-start | bytes 663556
  37.1 37.3 %copy-start.9 = (bf16[2,72,768]{2,1,0:T(8,128)(2,1)}, bf16[2,72,768]{2,1,0:T(8,128)(2,1)S(1)}, u32[]{:S(2)}) copy-start(bf16[2,72,768]{2,1,0:T(8,128)(2,1)S(1)} %get-tuple-element.90) | copy-start | bytes 663556
  37.1 37.3 %copy-start.10 = (bf16[2,72,768]{2,1,0:T(8,128)(2,1)}, bf16[2,72,768]{2,1,0:T(8,128)(2,1)S(1)}, u32[]{:S(2)}) copy-start(bf16[2,72,768]{2,1,0:T(8,128)(2,1)S(1)} %get-tuple-element.91) | copy-start | bytes 663556
  47.7 13.3 %collective-permute-start.7 = (bf16[288,768]{1,0:T(8,128)(2,1)S(1)}, bf16[288,768]{1,0:T(8,128)(2,1)S(1)}, u32[]{:S(2)}, u32[]{:S(2)}) collective-permute-start(bf16[288,768]{1,0:T(8,128)(2,1)S(1)} %collective-permute-done.5.refs_7_), channel_id=1, source_target_pairs={{0,32},{32,64},{64,96},{96,128},{128,160},{160,192},{192,224},{224... | collective-permute-start | bytes 1327112 | tf_op jit(solution)/shard_map/ppermute | solution.py:39
  47.7 13.3 %collective-permute-start.8 = (bf16[288,768]{1,0:T(8,128)(2,1)S(1)}, bf16[288,768]{1,0:T(8,128)(2,1)S(1)}, u32[]{:S(2)}, u32[]{:S(2)}) collective-permute-start(bf16[288,768]{1,0:T(8,128)(2,1)S(1)} %collective-permute-done.6.refs_8_), channel_id=1, source_target_pairs={{0,224},{32,0},{64,32},{96,64},{128,96},{160,128},{192,160},{224,1... | collective-permute-start | bytes 1327112 | tf_op jit(solution)/shard_map/ppermute | solution.py:39
  50.9 1.3 collective-permute-start.9
  61.0 12.7 %collective-permute-start.10 = (bf16[288,768]{1,0:T(8,128)(2,1)S(1)}, bf16[288,768]{1,0:T(8,128)(2,1)}, u32[]{:S(2)}, u32[]{:S(2)}) collective-permute-start(bf16[288,768]{1,0:T(8,128)(2,1)S(1)} %collective-permute-done.7.refs_9_), channel_id=1, source_target_pairs={{0,32},{32,64},{64,96},{96,128},{128,160},{160,192},{192,224},{224... | collective-permute-start | bytes 1327112 | tf_op jit(solution)/shard_map/ppermute | solution.py:39
  61.0 0.8 copy-start.1
  61.7 11.9 %collective-permute-start.11 = (bf16[288,768]{1,0:T(8,128)(2,1)S(1)}, bf16[288,768]{1,0:T(8,128)(2,1)S(1)}, u32[]{:S(2)}, u32[]{:S(2)}) collective-permute-start(bf16[288,768]{1,0:T(8,128)(2,1)S(1)} %collective-permute-done.8.refs_10_), channel_id=1, source_target_pairs={{0,224},{32,0},{64,32},{96,64},{128,96},{160,128},{192,160},{224,1... | collective-permute-start | bytes 1327112 | tf_op jit(solution)/shard_map/ppermute | solution.py:39
  65.0 0.8 copy-start.3
  65.8 5.4 %collective-permute-start.12 = (f32[2,3,768]{2,1,0:T(4,128)S(1)}, f32[2,3,768]{2,1,0:T(4,128)S(1)}, u32[]{:S(2)}, u32[]{:S(2)}) collective-permute-start(f32[2,3,768]{2,1,0:T(4,128)S(1)} %pad_maximum_fusion.4.refs_2_), channel_id=1, source_target_pairs={{0,16},{2,18},{16,0},{18,2},{1,17},{3,19},{17,1},{19,3},{4,20},{6,... | collective-permute-start | bytes 55304 | tf_op jit(solution)/shard_map/ppermute | solution.py:225
  67.0 4.2 %collective-permute-start.13 = (f32[2,3,768]{2,1,0:T(4,128)S(1)}, f32[2,3,768]{2,1,0:T(4,128)S(1)}, u32[]{:S(2)}, u32[]{:S(2)}) collective-permute-start(f32[2,3,768]{2,1,0:T(4,128)S(1)} %pad_maximum_fusion.4.refs_2_), channel_id=1, source_target_pairs={{0,2},{2,0},{16,18},{18,16},{1,3},{3,1},{17,19},{19,17},{4,6},{6,4... | collective-permute-start | bytes 55304 | tf_op jit(solution)/shard_map/ppermute | solution.py:225
  67.4 5.0 %collective-permute-start.14 = (f32[2,3,768]{2,1,0:T(4,128)S(1)}, f32[2,3,768]{2,1,0:T(4,128)S(1)}, u32[]{:S(2)}, u32[]{:S(2)}) collective-permute-start(f32[2,3,768]{2,1,0:T(4,128)S(1)} %pad_maximum_fusion.4.refs_2_), channel_id=1, source_target_pairs={{0,18},{2,16},{16,2},{18,0},{1,19},{3,17},{17,3},{19,1},{4,22},{6,... | collective-permute-start | bytes 55304 | tf_op jit(solution)/shard_map/ppermute | solution.py:225
  73.6 0.8 copy-start.5
  74.4 12.3 %collective-permute-start.15 = (bf16[288,768]{1,0:T(8,128)(2,1)}, bf16[288,768]{1,0:T(8,128)(2,1)}, u32[]{:S(2)}, u32[]{:S(2)}) collective-permute-start(bf16[288,768]{1,0:T(8,128)(2,1)} %collective-permute-done.10.refs_4_), channel_id=1, source_target_pairs={{0,32},{32,64},{64,96},{96,128},{128,160},{160,192},{192,224},{224... | collective-permute-start | bytes 1327112 | tf_op jit(solution)/shard_map/ppermute | solution.py:39
  76.2 2.3 %copy-start = (bf16[3072,768]{1,0:T(8,128)(2,1)S(1)}, bf16[3072,768]{1,0:T(8,128)(2,1)}, u32[]{:S(2)}) copy-start(bf16[3072,768]{1,0:T(8,128)(2,1)} %all-gather.3.cloned.1.call-done) | copy-start | bytes 14155780
  78.5 1.0 copy-start.2
  79.5 1.0 copy-start.4
  80.5 6.2 %copy-start.6 = (bf16[288,768]{1,0:T(8,128)(2,1)S(1)}, bf16[288,768]{1,0:T(8,128)(2,1)}, u32[]{:S(2)}) copy-start(bf16[288,768]{1,0:T(8,128)(2,1)} %copy-done.5) | copy-start | bytes 1327108
  90.5 1.3 collective-permute-start.16
  91.8 5.3 %collective-permute-start.17 = (f32[8,768]{1,0:T(8,128)S(1)}, f32[8,768]{1,0:T(8,128)S(1)}, u32[]{:S(2)}, u32[]{:S(2)}) collective-permute-start(f32[8,768]{1,0:T(8,128)S(1)} %add.112.refs_5_), channel_id=1, source_target_pairs={{0,16},{2,18},{16,0},{18,2},{1,17},{3,19},{17,1},{19,3},{4,20},{6,... | collective-permute-start | bytes 73736 | tf_op jit(solution)/shard_map/ppermute | solution.py:225
  92.3 5.4 %collective-permute-start.19 = (f32[8,768]{1,0:T(8,128)S(1)}, f32[8,768]{1,0:T(8,128)S(1)}, u32[]{:S(2)}, u32[]{:S(2)}) collective-permute-start(f32[8,768]{1,0:T(8,128)S(1)} %add.112.refs_5_), channel_id=1, source_target_pairs={{0,18},{2,16},{16,2},{18,0},{1,19},{3,17},{17,3},{19,1},{4,22},{6,... | collective-permute-start | bytes 73736 | tf_op jit(solution)/shard_map/ppermute | solution.py:225
  95.8 3.8 %collective-permute-start.18 = (f32[8,768]{1,0:T(8,128)S(1)}, f32[8,768]{1,0:T(8,128)S(1)}, u32[]{:S(2)}, u32[]{:S(2)}) collective-permute-start(f32[8,768]{1,0:T(8,128)S(1)} %add.112.refs_5_), channel_id=1, source_target_pairs={{0,2},{2,0},{16,18},{18,16},{1,3},{3,1},{17,19},{19,17},{4,6},{6,4... | collective-permute-start | bytes 73736 | tf_op jit(solution)/shard_map/ppermute | solution.py:225
  103.3 7.2 %collective-permute-start.20 = (bf16[144,768]{1,0:T(8,128)(2,1)S(1)}, bf16[144,768]{1,0:T(8,128)(2,1)S(1)}, u32[]{:S(2)}, u32[]{:S(2)}) collective-permute-start(bf16[144,768]{1,0:T(8,128)(2,1)S(1)} %get-tuple-element.66), channel_id=1, source_target_pairs={{0,32},{32,64},{64,96},{96,128},{128,160},{160,192},{192,224},{224... | collective-permute-start | bytes 663560 | tf_op jit(solution)/shard_map/ppermute | solution.py:39
  103.4 7.3 %collective-permute-start.24 = (bf16[144,768]{1,0:T(8,128)(2,1)S(1)}, bf16[144,768]{1,0:T(8,128)(2,1)S(1)}, u32[]{:S(2)}, u32[]{:S(2)}) collective-permute-start(bf16[144,768]{1,0:T(8,128)(2,1)S(1)} %get-tuple-element.74), channel_id=1, source_target_pairs={{0,224},{32,0},{64,32},{96,64},{128,96},{160,128},{192,160},{224,1... | collective-permute-start | bytes 663560 | tf_op jit(solution)/shard_map/ppermute | solution.py:39
  110.6 10.7 %collective-permute-start.21 = (bf16[288,768]{1,0:T(8,128)(2,1)S(1)}, bf16[288,768]{1,0:T(8,128)(2,1)S(1)}, u32[]{:S(2)}, u32[]{:S(2)}) collective-permute-start(bf16[288,768]{1,0:T(8,128)(2,1)S(1)} %pad_maximum_fusion.2), channel_id=1, source_target_pairs={{0,32},{32,64},{64,96},{96,128},{128,160},{160,192},{192,224},{224... | collective-permute-start | bytes 1327112 | tf_op jit(solution)/shard_map/ppermute | solution.py:39
  110.7 10.7 %collective-permute-start.25 = (bf16[288,768]{1,0:T(8,128)(2,1)S(1)}, bf16[288,768]{1,0:T(8,128)(2,1)S(1)}, u32[]{:S(2)}, u32[]{:S(2)}) collective-permute-start(bf16[288,768]{1,0:T(8,128)(2,1)S(1)} %pad_maximum_fusion.3), channel_id=1, source_target_pairs={{0,224},{32,0},{64,32},{96,64},{128,96},{160,128},{192,160},{224,1... | collective-permute-start | bytes 1327112 | tf_op jit(solution)/shard_map/ppermute | solution.py:39
  121.3 10.2 %collective-permute-start.22 = (bf16[288,768]{1,0:T(8,128)(2,1)S(1)}, bf16[288,768]{1,0:T(8,128)(2,1)S(1)}, u32[]{:S(2)}, u32[]{:S(2)}) collective-permute-start(bf16[288,768]{1,0:T(8,128)(2,1)S(1)} %add_convert_fusion.3), channel_id=1, source_target_pairs={{0,32},{32,64},{64,96},{96,128},{128,160},{160,192},{192,224},{224... | collective-permute-start | bytes 1327112 | tf_op jit(solution)/shard_map/ppermute | solution.py:39
  121.5 10.2 %collective-permute-start.26 = (bf16[288,768]{1,0:T(8,128)(2,1)S(1)}, bf16[288,768]{1,0:T(8,128)(2,1)S(1)}, u32[]{:S(2)}, u32[]{:S(2)}) collective-permute-start(bf16[288,768]{1,0:T(8,128)(2,1)S(1)} %add_convert_fusion.1), channel_id=1, source_target_pairs={{0,224},{32,0},{64,32},{96,64},{128,96},{160,128},{192,160},{224,1... | collective-permute-start | bytes 1327112 | tf_op jit(solution)/shard_map/ppermute | solution.py:39
  125.0 10.1 %collective-permute-start.32 = (bf16[2,4,72,384]{3,2,1,0:T(8,128)(2,1)S(1)}, bf16[2,4,72,384]{3,2,1,0:T(8,128)(2,1)}, u32[]{:S(2)}, u32[]{:S(2)}) collective-permute-start(bf16[2,4,72,384]{3,2,1,0:T(8,128)(2,1)S(1)} %slice.73), channel_id=1, source_target_pairs={{0,16},{16,0},{1,17},{17,1},{2,18},{18,2},{3,19},{19,3},{4,20},{20... | collective-permute-start | bytes 1327112 | tf_op jit(solution)/shard_map/ppermute | solution.py:39
  131.6 9.6 %collective-permute-start.23 = (bf16[288,768]{1,0:T(8,128)(2,1)S(1)}, bf16[288,768]{1,0:T(8,128)(2,1)S(1)}, u32[]{:S(2)}, u32[]{:S(2)}) collective-permute-start(bf16[288,768]{1,0:T(8,128)(2,1)S(1)} %add_convert_fusion.2), channel_id=1, source_target_pairs={{0,32},{32,64},{64,96},{96,128},{128,160},{160,192},{192,224},{224... | collective-permute-start | bytes 1327112 | tf_op jit(solution)/shard_map/ppermute | solution.py:39
  131.8 9.4 %collective-permute-start.27 = (bf16[288,768]{1,0:T(8,128)(2,1)S(1)}, bf16[288,768]{1,0:T(8,128)(2,1)}, u32[]{:S(2)}, u32[]{:S(2)}) collective-permute-start(bf16[288,768]{1,0:T(8,128)(2,1)S(1)} %add_convert_fusion), channel_id=1, source_target_pairs={{0,224},{32,0},{64,32},{96,64},{128,96},{160,128},{192,160},{224,1... | collective-permute-start | bytes 1327112 | tf_op jit(solution)/shard_map/ppermute | solution.py:39
  142.4 5.7 %collective-permute-start.28 = (bf16[72,768]{1,0:T(8,128)(2,1)S(1)}, bf16[72,768]{1,0:T(8,128)(2,1)S(1)}, u32[]{:S(2)}, u32[]{:S(2)}) collective-permute-start(bf16[72,768]{1,0:T(8,128)(2,1)S(1)} %get-tuple-element.94), channel_id=1, source_target_pairs={{0,12},{4,0},{8,4},{12,8},{1,13},{5,1},{9,5},{13,9},{2,14},{6,2},{... | collective-permute-start | bytes 331784 | tf_op jit(solution)/shard_map/ppermute | solution.py:39
  145.5 6.3 %collective-permute-start.29 = (bf16[72,768]{1,0:T(8,128)(2,1)S(1)}, bf16[72,768]{1,0:T(8,128)(2,1)S(1)}, u32[]{:S(2)}, u32[]{:S(2)}) collective-permute-start(bf16[72,768]{1,0:T(8,128)(2,1)S(1)} %get-tuple-element.96), channel_id=1, source_target_pairs={{0,8},{4,12},{8,0},{12,4},{1,9},{5,13},{9,1},{13,5},{2,10},{6,14},... | collective-permute-start | bytes 331784 | tf_op jit(solution)/shard_map/ppermute | solution.py:39
  146.1 6.8 %collective-permute-start.30 = (bf16[72,768]{1,0:T(8,128)(2,1)S(1)}, bf16[72,768]{1,0:T(8,128)(2,1)S(1)}, u32[]{:S(2)}, u32[]{:S(2)}) collective-permute-start(bf16[72,768]{1,0:T(8,128)(2,1)S(1)} %get-tuple-element.95), channel_id=1, source_target_pairs={{0,4},{4,8},{8,12},{12,0},{1,5},{5,9},{9,13},{13,1},{2,6},{6,10},{... | collective-permute-start | bytes 331784 | tf_op jit(solution)/shard_map/ppermute | solution.py:39
  153.0 11.4 %collective-permute-start.31 = (bf16[72,768]{1,0:T(8,128)(2,1)S(1)}, bf16[72,768]{1,0:T(8,128)(2,1)S(1)}, u32[]{:S(2)}, u32[]{:S(2)}) collective-permute-start(bf16[72,768]{1,0:T(8,128)(2,1)S(1)} %fusion), channel_id=1, source_target_pairs={{0,0},{64,1},{128,2},{192,3},{4,4},{68,5},{132,6},{196,7},{8,8},{7... | collective-permute-start | bytes 331784 | tf_op jit(solution)/shard_map/ppermute | solution.py:347
Sparse Core Ops, SparseCore 0:
  33.0 36.2 all-gather.2
